TPU v7x, 256 devices: a whole 4x4x8 slice. The times are simulated.
256 devices in a mesh: grp: 16 (over y, x_lo, core), dev: 16 (over z, x_hi).
Axes of the slice: x: 4 (x_hi: 2, x_lo: 2; x = x_hi * 2 + x_lo), y: 4, z: 8, core: 2. Of those that a mesh axis runs over, the one named last changes fastest.
Arguments:
- hidden: bfloat16 [49152, 2048], P(('grp', 'dev')), may hold values from -60 to 60
- weight: bfloat16 [2048, 128], replicated, may hold values from -0.125 to 0.125
- partner: int32 [49152], P(('grp', 'dev')), may hold values from 0 to 49151, as said below
Outputs:
- mean_loss: float32 [], replicated
- derivative_wrt_inputs: float32 [49152, 128], P(('grp', 'dev'))
- grad_weight: float32 [2048, 128], replicated
Inputs may be any that keep to these rules, and one draw needn't show every extreme that they name: partner[partner[i]] = i and partner[i] != i; partner[i] lies in the same aligned block of 192 rows as i.
All inputs are finite; a program needn't handle non-finite values.
Results may differ from a plain program's by a relative error of at most 0.0082.
Values may be sent and summed in bfloat16 or wider, within the bound.
No kernel may reach another device: no remote copies, remote signals or barrier semaphores. Data moves between devices by JAX's collectives and lax.ppermute only.
A program may use at most 128 MiB of HBM per device.

v0:
```python
import jax
import jax.numpy as jnp
from jax import lax
from jax.sharding import PartitionSpec as P

inverse_tau = 10.0
norm_epsilon = 1e-06


def paired_cosine(own_rows, leftover_entries):
    return inverse_tau * lax.dot_general(
        own_rows, leftover_entries, (((1,), (1,)), ((), ())), preferred_element_type=jnp.float32
    )


def scan_blocks(arrived, block_width, update, initial):
    block_count = arrived.shape[0] // block_width
    stacked = arrived.reshape(block_count, block_width, arrived.shape[1])

    def advance(running, element):
        position, segment = element
        return (update(running, segment, position * block_width), None)

    result, unused = lax.scan(advance, initial, (jnp.arange(block_count, dtype=jnp.int32), stacked))
    return result


def local(hidden, weight, partner):
    row_count = hidden.shape[0]
    projected = jnp.dot(hidden, weight, preferred_element_type=jnp.float32)
    inverse_norm = lax.rsqrt(jnp.sum(projected * projected, axis=1, keepdims=True) + norm_epsilon)
    unit_rows = projected * inverse_norm
    encoded_vectors = unit_rows.astype(jnp.bfloat16)
    partner_vectors = jnp.take(encoded_vectors, partner % row_count, axis=0).astype(jnp.float32)
    paired_scaled_score = inverse_tau * jnp.sum(
        encoded_vectors.astype(jnp.float32) * partner_vectors, axis=1
    )
    group_size = lax.axis_size("dev")
    group_count = lax.axis_size("grp")
    group_index = lax.axis_index("grp")
    group_rows = row_count * group_size
    own_ids = (group_index * group_size + lax.axis_index("dev")) * row_count + jnp.arange(
        row_count, dtype=jnp.int32
    )
    group_features = lax.all_gather(encoded_vectors, "dev", axis=0, tiled=True)
    sums_start = jnp.zeros((row_count,), jnp.float32)
    width_out = encoded_vectors.shape[1]

    def kept_indicator(first_row, column_count):
        return own_ids[:, None] != first_row + jnp.arange(column_count, dtype=jnp.int32)[None, :]

    def add_sums(running, leftover_entries, first_row):
        exponentiated = jnp.exp(paired_cosine(encoded_vectors, leftover_entries) - inverse_tau)
        exponentiated = jnp.where(
            kept_indicator(first_row, leftover_entries.shape[0]), exponentiated, 0.0
        )
        return running + jnp.sum(exponentiated, axis=1)

    device_partition_totals = scan_blocks(
        lax.all_gather(group_features, "grp", axis=0, tiled=True), group_rows, add_sums, sums_start
    )
    normalizer_logarithms = inverse_tau + jnp.log(device_partition_totals)
    group_logs = lax.all_gather(normalizer_logarithms, "dev", axis=0, tiled=True)

    def mixing_weights(leftover_entries, first_row, other_logs):
        scaled_cosine_matrix = paired_cosine(encoded_vectors, leftover_entries)
        combined = jnp.exp(scaled_cosine_matrix - normalizer_logarithms[:, None]) + jnp.exp(
            scaled_cosine_matrix - other_logs[None, :]
        )
        combined = jnp.where(kept_indicator(first_row, leftover_entries.shape[0]), combined, 0.0)
        return combined.astype(jnp.bfloat16)

    weighted_start = jnp.zeros((row_count, width_out), jnp.float32)
    every_log = lax.all_gather(group_logs, "grp", axis=0, tiled=True)

    def add_weighted(running, leftover_entries, first_row):
        other_logs = lax.dynamic_slice_in_dim(every_log, first_row, leftover_entries.shape[0], 0)
        mixing = mixing_weights(leftover_entries, first_row, other_logs)
        return running + jnp.dot(mixing, leftover_entries, preferred_element_type=jnp.float32)

    probability_combined_vector = scan_blocks(
        lax.all_gather(group_features, "grp", axis=0, tiled=True),
        group_rows,
        add_weighted,
        weighted_start,
    )
    derivative_wrt_inputs = inverse_tau * (probability_combined_vector - 2.0 * partner_vectors)
    alongside = jnp.sum(unit_rows * derivative_wrt_inputs, axis=1, keepdims=True)
    projected_grad = ((derivative_wrt_inputs - unit_rows * alongside) * inverse_norm).astype(
        jnp.bfloat16
    )
    local_grad = lax.dot_general(
        hidden, projected_grad, (((0,), (0,)), ((), ())), preferred_element_type=jnp.float32
    )
    grad_weight, loss_sum = lax.psum(
        (local_grad, jnp.sum(normalizer_logarithms - paired_scaled_score)), ("grp", "dev")
    )
    mean_loss = loss_sum / (row_count * group_size * group_count)
    return (mean_loss, derivative_wrt_inputs, grad_weight)


def solution(mesh):
    return jax.shard_map(
        local,
        mesh=mesh,
        in_specs=(P(("grp", "dev"), None), P(), P(("grp", "dev"))),
        out_specs=(P(), P(("grp", "dev"), None), P()),
        check_vma=False,
    )
```

profile of v0, /device:TPU:1, one launch (start us, length us, event | category | flops | bytes accessed | tf_op | source)
XLA Modules:
  0.0 604.5 jit_solution(15916686415667852846)
XLA Ops:
  9.9 44.2 %all_gather.13 = bf16[3072,128]{1,0:T(8,128)(2,1)} all-gather(bf16[192,128]{1,0:T(8,128)(2,1)S(1)} %multiply_convert_fusion.1), channel_id=1, replica_groups=mesh['grp'=16,'dev'=16] {'dev'}, dimensions={0}, use_global_device_ids=true | all-gather | bytes 835584 | tf_op jit(solution)/shard_map/all_gather | solution.py:45
  56.4 75.9 %all-gather.2.cloned.1.call-done = bf16[49152,128]{1,0:T(8,128)(2,1)} async-done(((bf16[3072,128]{1,0:T(8,128)(2,1)}), bf16[49152,128]{1,0:T(8,128)(2,1)}) %all-gather.2.cloned.1.call-update) | async-done | bytes 12582928 | tf_op jit(solution)/shard_map/all_gather | solution.py:60
  132.3 51.9 %while.24 = (s32[]{:T(128)}, f32[192]{0:T(256)S(1)}, s32[16]{0:T(128)S(1)}, bf16[16,3072,128]{2,1,0:T(8,128)(2,1)}, bf16[192,128]{1,0:T(8,128)(2,1)S(1)}, /*index=5*/s32[]{:T(128)}, s32[]{:T(128)}, s32[1]{0:T(128)}, s32[]{:T(128)}) while((s32[]{:T(128)}, f32[192]{0:T(256)S(1)}, s32[16]{0:T(128)S(1)}, ...), condition=%wide.region_3.4_spmd.clone, body=%wide.region_1.3_spmd.clone.sunk | while | flops 153947520 | bytes 865415 | solution.py:24
  184.4 63.3 %all-reduce = f32[3072]{0:T(1024)S(1)} all-reduce(f32[3072]{0:T(1024)S(1)} %get-tuple-element.217), channel_id=1, replica_groups=mesh['grp'=16,'dev'=16] {'dev'}, use_global_device_ids=true, to_apply=%add | all-reduce | flops 3072 | bytes 24576
  247.7 33.0 %all_gather.16 = f32[49152]{0:T(1024)S(1)} all-gather(f32[3072]{0:T(1024)S(1)} %all-reduce), channel_id=1, replica_groups=mesh['grp'=16,'dev'=16] {'grp'}, dimensions={0}, use_global_device_ids=true | all-gather | bytes 208896 | tf_op jit(solution)/shard_map/all_gather | solution.py:74
  280.7 63.5 %while.25 = (s32[]{:T(128)}, f32[192,128]{1,0:T(8,128)S(1)}, s32[16]{0:T(128)S(1)}, bf16[16,3072,128]{2,1,0:T(8,128)(2,1)}, bf16[192,128]{1,0:T(8,128)(2,1)S(1)}...) while((s32[]{:T(128)}, f32[192,128]{1,0:T(8,128)S(1)}, ...), condition=%wide.region_8.9_spmd.clone, body=%wide.region_7.8_spmd.clone.sunk | while | flops 306171072 | bytes 1883589 | solution.py:24
  282.0 2.6 fusion.54
  285.9 2.6 fusion.54
  289.9 2.6 fusion.54
  293.9 2.6 fusion.54
  297.8 2.6 fusion.54
  301.7 2.6 fusion.54
  305.7 2.7 fusion.54
  309.7 2.7 fusion.54
  313.7 2.6 fusion.54
  317.7 2.6 fusion.54
  321.6 2.8 fusion.54
  325.7 2.7 fusion.54
  329.7 2.6 fusion.54
  333.6 2.6 fusion.54
  337.6 2.7 fusion.54
  341.6 2.6 fusion.54
  346.5 73.0 %psum.14 = f32[]{:T(128)} all-reduce(f32[]{:T(128)} %subtract_reduce_fusion), channel_id=1, replica_groups=mesh['grp'=16,'dev'=16] {'grp','dev'}, use_global_device_ids=true, to_apply=%region_6.7 | all-reduce | flops 1 | bytes 8 | tf_op jit(solution)/shard_map/psum | solution.py:95
  420.1 173.8 %all-reduce.3.cloned.1.call-done = f32[2048,128]{0,1:T(8,128)} async-done(((f32[2048,128]{0,1:T(8,128)}), f32[2048,128]{0,1:T(8,128)}) %all-reduce.3.cloned.1.call-update) | async-done | bytes 1048592 | tf_op jit(solution)/shard_map/psum | solution.py:95
  (173 shorter events, 60.5 us)
Async XLA Ops:
  7.2 1.2 copy-start
  7.2 47.9 %copy-start.3 = (u32[256]{0:T(256)S(1)}, u32[256]{0:T(256)}, u32[]{:S(2)}) copy-start(u32[256]{0:T(256)} %constant.105) | copy-start | bytes 3076
  7.2 47.1 %copy-start.2 = (s32[192]{0:T(256)S(1)}, s32[192]{0:T(256)}, u32[]{:S(2)}) copy-start(s32[192]{0:T(256)} %param.9) | copy-start | bytes 2308
  7.2 125.1 %all-gather.2.cloned.1.call-start = ((), (), s32[]{:S(2)}) async-start(), calls=%async_computation | async-start | bytes 13369344 | tf_op jit(solution)/shard_map/all_gather | solution.py:60
  54.2 539.8 %all-reduce.3.cloned.1.call-start = ((), (), s32[]{:S(2)}) async-start(), calls=%async_computation.1 | async-start | bytes 2097152 | tf_op jit(solution)/shard_map/psum | solution.py:95
  344.5 252.0 %copy-start.1 = (f32[192,128]{1,0:T(8,128)}, f32[192,128]{1,0:T(8,128)S(1)}, u32[]{:S(2)}) copy-start(f32[192,128]{1,0:T(8,128)S(1)} %get-tuple-element.213) | copy-start | bytes 294916
Sparse Core Ops, SparseCore 0:
  54.3 77.9 all-gather.1
  346.0 247.9 all-reduce.2
where the time goes:
time: 607 us; the launch traced here: 604 us
  waiting for transfers between devices  250 us (41%)
  blocking collectives  214 us (35%)
  matrix products  76.7 us (13%)
  local copies, waits for them, and re-layouts  24.4 us (4%)
  loops' own time  21.6 us (4%)
  between operations  16.6 us (3%)
    psum x1, waiting for transfers between devices, local(): lax.psum((local_grad, jnp.sum(normalizer_logarithms - paired_scaled_score...  174 us
    all_gather x1, waiting for transfers between devices, local(): lax.all_gather(group_features, 'grp', axis=0, tiled=True)  75.9 us
    psum x1, blocking collectives, local(): lax.psum((local_grad, jnp.sum(normalizer_logarithms - paired_scaled_score...  73 us
    unnamed x1, blocking collectives  63.3 us
    all_gather x1, blocking collectives, local(): group_features = lax.all_gather(encoded_vectors, 'dev', axis=0, tiled=True)  44.2 us
    dot_general x16, matrix products, add_weighted(): jnp.dot(mixing, leftover_entries, preferred_element_type=jnp.float32)  42.5 us
    all_gather x1, blocking collectives, local(): every_log = lax.all_gather(group_logs, 'grp', axis=0, tiled=True)  33 us
    dot_general x16, matrix products, paired_cosine(): lax.dot_general(own_rows, leftover_entries, (((1,), (1,)), ((), ())), pre...  31.4 us
  transfers between devices with their start and end apart: 2, of which 2 were waited for; matrix products, arithmetic and copies ran while one was open for 0% of the time, Pallas kernels for 0%

commit v1 on v0

v1 whole, which is shorter than its diff:
```python
import jax
import jax.numpy as jnp
from jax import lax
from jax.experimental import pallas as pl
from jax.experimental.pallas import tpu as pltpu
from jax.sharding import Mesh
from jax.sharding import PartitionSpec as P

inverse_tau = 10.0
norm_epsilon = 1e-06
log2_e = 1.4426950408889634

AXES = ("y", "xl", "c", "z", "xh")
PLANE = ("y", "xl", "xh")
ROWS = 192
WIDTH = 128
D_IN = 2048
HALF = 8 * ROWS
SPAN = 16 * ROWS
BLOCK = 384
CHUNK = 256
VMEM_BYTES = 56 * 1024 * 1024


def params():
    return pltpu.CompilerParams(vmem_limit_bytes=VMEM_BYTES)


def whole(shape):
    return pl.BlockSpec(shape, lambda *_: (0,) * len(shape))


def project_body(hidden_ref, weight_ref, partner_ref, projected_ref, features_ref, pair_ref, pair_sum_ref):
    projected = jnp.dot(hidden_ref[...], weight_ref[...], preferred_element_type=jnp.float32)
    inverse_norm = lax.rsqrt(jnp.sum(projected * projected, axis=1, keepdims=True) + norm_epsilon)
    features = (projected * inverse_norm).astype(jnp.bfloat16)
    places = lax.rem(partner_ref[...], ROWS)
    picks = lax.broadcasted_iota(jnp.int32, (ROWS, ROWS), 0) == places
    paired = jnp.dot(
        jnp.where(picks, 1.0, 0.0).astype(jnp.bfloat16), features, preferred_element_type=jnp.float32
    )
    projected_ref[...] = projected
    features_ref[...] = features
    pair_ref[...] = paired
    products = features.astype(jnp.float32) * paired
    total = jnp.sum(jnp.sum(products, axis=1, keepdims=True), axis=0, keepdims=True)
    pair_sum_ref[...] = jnp.broadcast_to(inverse_tau * total, (8, WIDTH))


def project(hidden, weight, partner):
    return pl.pallas_call(
        project_body,
        out_shape=(
            jax.ShapeDtypeStruct((ROWS, WIDTH), jnp.float32),
            jax.ShapeDtypeStruct((ROWS, WIDTH), jnp.bfloat16),
            jax.ShapeDtypeStruct((ROWS, WIDTH), jnp.float32),
            jax.ShapeDtypeStruct((8, WIDTH), jnp.float32),
        ),
        compiler_params=params(),
        name="project",
    )(hidden, weight, partner.reshape(1, ROWS))


def score_body(place_ref, own_ref, other_ref, columns_ref, pair_sum_ref, powers_ref, sums_ref, turned, running):
    step = pl.program_id(0)
    own_steps = HALF // BLOCK

    @pl.when(step == 0)
    def _():
        for n in range(SPAN // CHUNK):
            piece = jnp.transpose(columns_ref[pl.ds(n * CHUNK, CHUNK), :])
            turned[0:WIDTH, pl.ds(n * CHUNK, CHUNK)] = piece
            turned[WIDTH : 2 * WIDTH, pl.ds(n * CHUNK, CHUNK)] = piece
        running[...] = jnp.zeros_like(running)

    first = lax.rem(step, own_steps) * BLOCK
    rows = jnp.where(
        step < own_steps,
        own_ref[pl.ds(first, BLOCK), :].astype(jnp.float32),
        other_ref[pl.ds(first, BLOCK), :].astype(jnp.float32),
    )
    scaled = rows * (inverse_tau * log2_e)
    high = scaled.astype(jnp.bfloat16)
    low = (scaled - high.astype(jnp.float32)).astype(jnp.bfloat16)
    left = jnp.concatenate([high, low], axis=1)

    def fill(masked):
        for n in range(SPAN // CHUNK):
            columns = pl.ds(n * CHUNK, CHUNK)
            powers = jnp.exp2(jnp.dot(left, turned[:, columns], preferred_element_type=jnp.float32))
            if masked:
                own_row = first + lax.broadcasted_iota(jnp.int32, (BLOCK, CHUNK), 0) - place_ref[0] * ROWS
                own_column = n * CHUNK + lax.broadcasted_iota(jnp.int32, (BLOCK, CHUNK), 1) - place_ref[1] * ROWS
                same = (own_row == own_column) & (own_row >= 0) & (own_row < ROWS)
                powers = jnp.where(same, 0.0, powers)
            powers_ref[:, columns] = powers.astype(jnp.bfloat16)
            running[:, columns] += jnp.sum(powers.reshape(BLOCK // 8, 8, CHUNK), axis=0)

    masked_step = (step < own_steps) & (first <= place_ref[0] * ROWS) & (place_ref[0] * ROWS < first + BLOCK)
    pl.when(masked_step)(lambda: fill(True))
    pl.when(jnp.logical_not(masked_step))(lambda: fill(False))

    @pl.when(step == pl.num_programs(0) - 1)
    def _():
        sums = jnp.sum(running[...], axis=0, keepdims=True)
        for k in range(SPAN // WIDTH):
            sums_ref[k : k + 1, :] = sums[:, k * WIDTH : (k + 1) * WIDTH]
        sums_ref[SPAN // WIDTH :, :] = pair_sum_ref[...]


def score(place, own, other, columns, pair_sum):
    return pl.pallas_call(
        score_body,
        grid=(SPAN // BLOCK,),
        in_specs=[
            pl.BlockSpec(memory_space=pltpu.SMEM),
            whole((HALF, WIDTH)),
            whole((HALF, WIDTH)),
            whole((SPAN, WIDTH)),
            whole((8, WIDTH)),
        ],
        out_specs=(
            pl.BlockSpec((BLOCK, SPAN), lambda i: (i, 0)),
            whole((SPAN // WIDTH + 8, WIDTH)),
        ),
        out_shape=(
            jax.ShapeDtypeStruct((SPAN, SPAN), jnp.bfloat16),
            jax.ShapeDtypeStruct((SPAN // WIDTH + 8, WIDTH), jnp.float32),
        ),
        scratch_shapes=[
            pltpu.VMEM((2 * WIDTH, SPAN), jnp.bfloat16),
            pltpu.VMEM((8, SPAN), jnp.float32),
        ],
        compiler_params=params(),
        name="score",
    )(place, own, other, columns, pair_sum)


def weigh_other_body(place_ref, partial_ref, columns_ref, powers_ref, out_ref, both_ref, own_ref, loss_ref, inverse):
    @pl.when(pl.program_id(0) == 0)
    def _():
        tiles = SPAN // WIDTH
        sums = jnp.sum(partial_ref[...], axis=0)
        totals = sums[:tiles, :]
        loss = jnp.sum(jnp.sum(jnp.log(totals), axis=1, keepdims=True), axis=0, keepdims=True)
        loss_ref[...] = loss - sums[tiles:, :]
        inverses = 1.0 / totals
        for k in range(tiles):
            rows = pl.ds(k * WIDTH, WIDTH)
            turned = jnp.transpose(jnp.broadcast_to(inverses[k : k + 1, :], (WIDTH, WIDTH)))
            inverse[rows, :] = turned
            piece = columns_ref[rows, :]
            both_ref[rows, 0:WIDTH] = piece
            both_ref[rows, WIDTH : 2 * WIDTH] = (piece.astype(jnp.float32) * turned).astype(jnp.bfloat16)
        own_ref[...] = inverse[pl.ds(pl.multiple_of(place_ref[1] * ROWS, ROWS), ROWS), :]

    out_ref[...] = jnp.dot(
        powers_ref[...], both_ref[...], preferred_element_type=jnp.float32
    ).astype(jnp.bfloat16)


def weigh_other(place, partial, columns, powers):
    return pl.pallas_call(
        weigh_other_body,
        grid=(HALF // BLOCK,),
        in_specs=[
            pl.BlockSpec(memory_space=pltpu.SMEM),
            whole(partial.shape),
            whole((SPAN, WIDTH)),
            pl.BlockSpec((BLOCK, SPAN), lambda i: (i + HALF // BLOCK, 0)),
        ],
        out_specs=(
            pl.BlockSpec((BLOCK, 2 * WIDTH), lambda i: (i, 0)),
            whole((SPAN, 2 * WIDTH)),
            whole((ROWS, WIDTH)),
            whole((8, WIDTH)),
        ),
        out_shape=(
            jax.ShapeDtypeStruct((HALF, 2 * WIDTH), jnp.bfloat16),
            jax.ShapeDtypeStruct((SPAN, 2 * WIDTH), jnp.bfloat16),
            jax.ShapeDtypeStruct((ROWS, WIDTH), jnp.float32),
            jax.ShapeDtypeStruct((8, WIDTH), jnp.float32),
        ),
        scratch_shapes=[pltpu.VMEM((SPAN, WIDTH), jnp.float32)],
        compiler_params=params(),
        name="weigh_other",
    )(place, partial, columns, powers)


def weigh_own_body(both_ref, powers_ref, out_ref):
    out_ref[...] = jnp.dot(powers_ref[...], both_ref[...], preferred_element_type=jnp.float32)


def weigh_own(both, powers):
    return pl.pallas_call(
        weigh_own_body,
        grid=(HALF // BLOCK,),
        in_specs=[
            whole((SPAN, 2 * WIDTH)),
            pl.BlockSpec((BLOCK, SPAN), lambda i: (i, 0)),
        ],
        out_specs=pl.BlockSpec((BLOCK, 2 * WIDTH), lambda i: (i, 0)),
        out_shape=jax.ShapeDtypeStruct((HALF, 2 * WIDTH), jnp.float32),
        compiler_params=params(),
        name="weigh_own",
        cost_estimate=pl.CostEstimate(
            flops=2 * HALF * SPAN * 2 * WIDTH, bytes_accessed=2 * HALF * SPAN, transcendentals=0
        ),
    )(both, powers)


def gradient_body(core_ref, arrived_ref, inverse_ref, pair_ref, projected_ref, hidden_ref, derivative_ref, own_ref, other_ref):
    sums = jnp.sum(arrived_ref[...].astype(jnp.float32), axis=0)
    mixed = inverse_ref[...] * sums[:, :WIDTH] + sums[:, WIDTH:]
    derivative = inverse_tau * (mixed - 2.0 * pair_ref[...])
    derivative_ref[...] = derivative
    projected = projected_ref[...]
    inverse_norm = lax.rsqrt(jnp.sum(projected * projected, axis=1, keepdims=True) + norm_epsilon)
    unit = projected * inverse_norm
    alongside = jnp.sum(unit * derivative, axis=1, keepdims=True)
    projected_grad = ((derivative - unit * alongside) * inverse_norm).astype(jnp.bfloat16)
    share = D_IN // 2
    for half in range(2):
        product = lax.dot_general(
            hidden_ref[:, half * share : (half + 1) * share],
            projected_grad,
            (((0,), (0,)), ((), ())),
            preferred_element_type=jnp.float32,
        )

        @pl.when(core_ref[0] == half)
        def _():
            own_ref[...] = product

        @pl.when(core_ref[0] != half)
        def _():
            other_ref[...] = product.astype(jnp.bfloat16)


def gradient(core, arrived, inverse, pair, projected, hidden):
    vmem = pl.BlockSpec(memory_space=pltpu.VMEM)
    return pl.pallas_call(
        gradient_body,
        in_specs=[pl.BlockSpec(memory_space=pltpu.SMEM)] + [vmem] * 5,
        out_shape=(
            jax.ShapeDtypeStruct((ROWS, WIDTH), jnp.float32),
            jax.ShapeDtypeStruct((D_IN // 2, WIDTH), jnp.float32),
            jax.ShapeDtypeStruct((D_IN // 2, WIDTH), jnp.bfloat16),
        ),
        compiler_params=params(),
        name="gradient",
    )(core, arrived, inverse, pair, projected, hidden)


def swapped(value):
    return lax.ppermute(value, "c", [(0, 1), (1, 0)])


def spread(value, axes, count):
    copies = jnp.broadcast_to(value[None], (count, *value.shape))
    return lax.all_to_all(copies, axes, 0, 0)


def local(hidden, weight, partner):
    core = lax.axis_index("c").astype(jnp.int32).reshape(1)
    plane_place = (lax.axis_index("y") * 2 + lax.axis_index("xl")) * 2 + lax.axis_index("xh")
    place = jnp.stack([lax.axis_index("z"), plane_place]).astype(jnp.int32)

    projected, features, pair, pair_sum = project(hidden, weight, partner)
    own = spread(features, "z", 8).reshape(HALF, WIDTH)
    other = swapped(own)
    columns = spread(features, PLANE, 16).reshape(SPAN, WIDTH)

    powers, sums = score(place, own, other, columns, pair_sum)
    partial = spread(sums, PLANE, 16)
    other_weighed, both, inverse, loss = weigh_other(place, partial, columns, powers)
    other_arrived = swapped(other_weighed)
    loss = loss + swapped(loss)
    own_weighed = weigh_own(both, powers)
    combined = (own_weighed + other_arrived.astype(jnp.float32)).astype(jnp.bfloat16)
    arrived = lax.all_to_all(combined.reshape(8, ROWS, 2 * WIDTH), "z", 0, 0)

    derivative, own_grad, other_grad = gradient(core, arrived, inverse, pair, projected, hidden)
    half_grad = (own_grad + swapped(other_grad).astype(jnp.float32)).astype(jnp.bfloat16)
    shares = lax.all_to_all(half_grad.reshape(16, 64, WIDTH), PLANE, 0, 0)
    share = jnp.sum(shares.astype(jnp.float32), axis=0)
    summed = jnp.sum(spread(jnp.concatenate([share, loss], axis=0), "z", 8), axis=0)
    mean_loss = summed[64, 0] / (256 * ROWS)
    own_part = spread(summed[:64].astype(jnp.bfloat16), PLANE, 16).reshape(D_IN // 2, WIDTH)
    other_part = swapped(own_part)
    first = jnp.where(core[0] == 0, own_part, other_part)
    second = jnp.where(core[0] == 0, other_part, own_part)
    grad_weight = jnp.concatenate([first, second], axis=0).astype(jnp.float32)
    return (mean_loss, derivative, grad_weight)


def solution(mesh):
    split = Mesh(mesh.devices.reshape(4, 2, 2, 8, 2), AXES)
    return jax.shard_map(
        local,
        mesh=split,
        in_specs=(P(AXES, None), P(), P(AXES)),
        out_specs=(P(), P(AXES, None), P()),
        check_vma=False,
    )
```

time: 607 us -> 172 us (0.28)
  waiting for transfers between devices: 250 us -> 39.3 us
  blocking collectives: 214 us -> 58.4 us
  matrix products: 76.7 us -> 0 us
  Pallas kernels: 0 us -> 33.4 us
  starting transfers between devices: 0.08 us -> 25.4 us
  loops' own time: 21.6 us -> 0 us
  local copies, waits for them, and re-layouts: 24.4 us -> 5.91 us
  between operations: 16.6 us -> 2.53 us
    psum x1 -> x0, waiting for transfers between devices: 174 us -> none  [local(): lax.psum((local_grad, jnp.sum(normalizer_logarithms - paired_scaled_score...]
    all_gather x2 -> x0, blocking collectives: 77.3 us -> none  [the longest x1 44.2 us: local(): group_features = lax.all_gather(encoded_vectors, 'dev', axis=0, tiled=True)]
    dot_general x34 -> x0, matrix products: 76.7 us -> none  [the longest x16 42.5 us: add_weighted(): jnp.dot(mixing, leftover_entries, preferred_element_type=jnp.float32)]
    all_gather x1 -> x0, waiting for transfers between devices: 75.9 us -> none  [local(): lax.all_gather(group_features, 'grp', axis=0, tiled=True)]
    psum x1 -> x0, blocking collectives: 73 us -> none  [local(): lax.psum((local_grad, jnp.sum(normalizer_logarithms - paired_scaled_score...]
    unnamed x1 -> x0, blocking collectives: 63.3 us -> none
    all_to_all x0 -> x4, blocking collectives: none -> 58.4 us  [spread(): return lax.all_to_all(copies, axes, 0, 0)]
    all_to_all x0 -> x3, waiting for transfers between devices: none -> 37.1 us  [the longest x1 23.6 us: local(): arrived = lax.all_to_all(combined.reshape(8, ROWS, 2 * WIDTH), 'z', 0, 0)]
  transfers between devices with their start and end apart: 2 -> 8, of which waited for: 2 -> 5; matrix products, arithmetic and copies ran while one was open for 0% -> 1% of each run, Pallas kernels for 0% -> 4%
where the time goes in v1:
time: 172 us; the launch traced here: 171 us
  blocking collectives  58.4 us (34%)
  waiting for transfers between devices  39.3 us (23%)
  Pallas kernels  33.4 us (19%)
  starting transfers between devices  25.4 us (15%)
  other arithmetic  6.05 us (4%)
  local copies, waits for them, and re-layouts  5.91 us (3%)
  between operations  2.53 us (1%)
    all_to_all x4, blocking collectives, spread(): return lax.all_to_all(copies, axes, 0, 0)  58.4 us
    all_to_all x1, waiting for transfers between devices, local(): arrived = lax.all_to_all(combined.reshape(8, ROWS, 2 * WIDTH), 'z', 0, 0)  23.6 us
    pallas_call x1, Pallas kernels, score(): pl.pallas_call(score_body, grid=(SPAN // BLOCK,), in_specs=[pl.BlockSpec(...  12.6 us
    ppermute x5, starting transfers between devices, swapped(): return lax.ppermute(value, 'c', [(0, 1), (1, 0)])  11.6 us
    all_to_all x1, waiting for transfers between devices, spread(): return lax.all_to_all(copies, axes, 0, 0)  7.49 us
    pallas_call x1, Pallas kernels, weigh_other(): pl.pallas_call(weigh_other_body, grid=(HALF // BLOCK,), in_specs=[pl.Bloc...  7.48 us
    pallas_call x1, Pallas kernels, weigh_own(): pl.pallas_call(weigh_own_body, grid=(HALF // BLOCK,), in_specs=[whole((SP...  7.22 us
    all_to_all x1, starting transfers between devices, spread(): return lax.all_to_all(copies, axes, 0, 0)  6.76 us
  transfers between devices with their start and end apart: 8, of which 5 were waited for; matrix products, arithmetic and copies ran while one was open for 1% of the time, Pallas kernels for 4%

profile of v1, /device:TPU:1, one launch (start us, length us, event | category | flops | bytes accessed | tf_op | source)
XLA Modules:
  0.0 171.0 jit_solution(12377597375999167563)
XLA Ops:
  0.6 2.6 %project.1 = (f32[192,128]{1,0:T(8,128)}, bf16[192,128]{1,0:T(8,128)(2,1)}, f32[192,128]{1,0:T(8,128)}, f32[8,128]{1,0:T(8,128)}) custom-call(bf16[192,2048]{1,0:T(8,128)(2,1)} %hidden_ref.3, bf16[2048,128]{1,0:T(8,128)(2,1)} %weight_ref.1, s32[1,192]{1,0:T(1,128)} %bitcast.17), custom_call_target="tpu_custom_call" | custom-call | tf_op jit(solution)/shard_map/project/pallas_call | solution.py:51
  4.1 22.3 %all_to_all.35 = bf16[8,192,128]{2,1,0:T(8,128)(2,1)S(1)} all-to-all(bf16[8,192,128]{2,1,0:T(8,128)(2,1)S(1)} %broadcast_in_dim.10), channel_id=1, replica_groups=mesh['y'=4,'xl'=2,'c'=2,'z'=8,'xh'=2] {'z'}, dimensions={0} | all-to-all | bytes 786432 | tf_op jit(solution)/shard_map/all_to_all | solution.py:261
  26.4 1.9 %broadcast_in_dim.11 = bf16[16,192,128]{2,1,0:T(8,128)(2,1)} broadcast(bf16[192,128]{1,0:T(8,128)(2,1)} %get-tuple-element.16), dimensions={1,2} | broadcast | bytes 835584 | tf_op jit(solution)/shard_map/broadcast_in_dim | solution.py:260
  28.3 6.8 %all-to-all-start.1 = ((bf16[16,192,128]{2,1,0:T(8,128)(2,1)}), bf16[16,192,128]{2,1,0:T(8,128)(2,1)S(1)}, u32[]{:S(2)}, u32[]{:S(2)}) async-start(bf16[16,192,128]{2,1,0:T(8,128)(2,1)} %broadcast_in_dim.11), calls=%async_computation.1 | async-start | bytes 1572864 | tf_op jit(solution)/shard_map/all_to_all | solution.py:261
  35.0 2.5 %collective-permute-start = (bf16[1536,128]{1,0:T(8,128)(2,1)S(1)}, bf16[1536,128]{1,0:T(8,128)(2,1)S(1)}, u32[]{:S(2)}, u32[]{:S(2)}) collective-permute-start(bf16[1536,128]{1,0:T(8,128)(2,1)S(1)} %bitcast.14), channel_id=1, source_target_pairs={{0,16},{16,0},{1,17},{17,1},{2,18},{18,2},{3,19},{19,3},{4,20},{20... | collective-permute-start | bytes 1179656 | tf_op jit(solution)/shard_map/ppermute | solution.py:256
  38.1 7.5 %all-to-all-done.1 = bf16[16,192,128]{2,1,0:T(8,128)(2,1)S(1)} async-done(((bf16[16,192,128]{2,1,0:T(8,128)(2,1)}), bf16[16,192,128]{2,1,0:T(8,128)(2,1)S(1)}, u32[]{:S(2)}, u32[]{:S(2)}) %all-to-all-start.1) | async-done | bytes 786464 | tf_op jit(solution)/shard_map/all_to_all | solution.py:261
  46.6 12.6 %score.1 = (bf16[3072,3072]{1,0:T(8,128)(2,1)}, f32[32,128]{1,0:T(8,128)}) custom-call(s32[2]{0:T(128)} %pad_add_fusion.place_ref, bf16[1536,128]{1,0:T(8,128)(2,1)} %bitcast.15, bf16[1536,128]{1,0:T(8,128)(2,1)} %copy-done.3, bf16[3072,128]{1,0:T(8,128)(2,1)} %bitcast.12, f32[8,128]{1,0:T(8,128)} %get-tuple-element.17.pair_sum_ref), custom_call_target="tpu_custom_call" | custom-call | tf_op jit(solution)/shard_map/score/pallas_call | solution.py:112
  59.9 12.3 %all_to_all.36.partial_ref = f32[16,32,128]{2,1,0:T(8,128)} all-to-all(f32[16,32,128]{2,1,0:T(8,128)S(1)} %broadcast_in_dim.12), channel_id=1, replica_groups=mesh['y'=4,'xl'=2,'c'=2,'z'=8,'xh'=2] {'y','xl','xh'}, dimensions={0} | all-to-all | bytes 524288 | tf_op jit(solution)/shard_map/all_to_all | solution.py:261
  72.3 7.5 %weigh_other.1 = (bf16[1536,256]{1,0:T(8,128)(2,1)}, bf16[3072,256]{1,0:T(8,128)(2,1)}, f32[192,128]{1,0:T(8,128)}, f32[8,128]{1,0:T(8,128)}) custom-call(s32[2]{0:T(128)} %pad_add_fusion.place_ref, f32[16,32,128]{2,1,0:T(8,128)} %all_to_all.36.partial_ref, bf16[3072,128]{1,0:T(8,128)(2,1)} %bitcast.13, bf16[3072,3072]{1,0:T(8,128)(2,1)} %get-tuple-element.19.powers_ref), custom_call_target="tpu_custom_call" | custom-call | tf_op jit(solution)/shard_map/weigh_other/pallas_call | solution.py:163
  79.7 3.7 %collective-permute-start.1 = (bf16[1536,256]{1,0:T(8,128)(2,1)}, bf16[1536,256]{1,0:T(8,128)(2,1)S(1)}, u32[]{:S(2)}, u32[]{:S(2)}) collective-permute-start(bf16[1536,256]{1,0:T(8,128)(2,1)} %get-tuple-element.21), channel_id=1, source_target_pairs={{0,16},{16,0},{1,17},{17,1},{2,18},{18,2},{3,19},{19,3},{4,20},{20... | collective-permute-start | bytes 2359304 | tf_op jit(solution)/shard_map/ppermute | solution.py:256
  83.4 7.2 %weigh_own.1 = f32[1536,256]{1,0:T(8,128)} custom-call(bf16[3072,256]{1,0:T(8,128)(2,1)} %get-tuple-element.20.both_ref, bf16[3072,3072]{1,0:T(8,128)(2,1)} %get-tuple-element.19.powers_ref), custom_call_target="tpu_custom_call" | custom-call | flops 2415919104 | bytes 9437184 | tf_op jit(solution)/shard_map/weigh_own/pallas_call | solution.py:195
  90.6 2.5 %add_convert_fusion = bf16[1536,256]{1,0:T(8,128)(2,1)} fusion(f32[1536,256]{1,0:T(8,128)} %weigh_own.1, bf16[1536,256]{1,0:T(8,128)(2,1)S(1)} %collective-permute-done.1), kind=kLoop, calls=%fused_computation | loop fusion | flops 1179648 | bytes 3145728 | tf_op jit(solution)/shard_map/convert_element_type | solution.py:280
  93.1 3.5 %all-to-all-start.3 = ((bf16[8,192,256]{2,1,0:T(8,128)(2,1)}), bf16[8,192,256]{2,1,0:T(8,128)(2,1)S(1)}, u32[]{:S(2)}, u32[]{:S(2)}) async-start(bf16[8,192,256]{2,1,0:T(8,128)(2,1)} %bitcast.6), calls=%async_computation.3 | async-start | bytes 1572864 | tf_op jit(solution)/shard_map/all_to_all | solution.py:281
  96.7 23.6 %all-to-all-done.3.arrived_ref = bf16[8,192,256]{2,1,0:T(8,128)(2,1)S(1)} async-done(((bf16[8,192,256]{2,1,0:T(8,128)(2,1)}), bf16[8,192,256]{2,1,0:T(8,128)(2,1)S(1)}, u32[]{:S(2)}, u32[]{:S(2)}) %all-to-all-start.3) | async-done | bytes 786464 | tf_op jit(solution)/shard_map/all_to_all | solution.py:281
  120.2 0.9 copy-done.1
  121.1 3.5 %gradient.1 = (f32[192,128]{1,0:T(8,128)}, f32[1024,128]{1,0:T(8,128)}, bf16[1024,128]{1,0:T(8,128)(2,1)}) custom-call(s32[1]{0:T(128)} %bitcast.core_ref, bf16[8,192,256]{2,1,0:T(8,128)(2,1)} %copy-done.1, f32[192,128]{1,0:T(8,128)} %get-tuple-element.22.inverse_ref, f32[192,128]{1,0:T(8,128)} %get-tuple-element.23.pair_ref, ...), custom_call_target="tpu_custom_call" | custom-call | tf_op jit(solution)/shard_map/gradient/pallas_call | solution.py:242
  125.1 1.4 collective-permute-done.2
  126.5 1.8 %add_convert_fusion.1 = bf16[1024,128]{1,0:T(8,128)(2,1)} fusion(f32[1024,128]{1,0:T(8,128)} %get-tuple-element.25, bf16[1024,128]{1,0:T(8,128)(2,1)S(1)} %collective-permute-done.2), kind=kLoop, calls=%fused_computation.3 | loop fusion | flops 393216 | bytes 1048576 | tf_op jit(solution)/shard_map/convert_element_type | solution.py:284
  128.3 3.5 %all-to-all-start.4 = ((bf16[16,64,128]{2,1,0:T(8,128)(2,1)}), bf16[16,64,128]{2,1,0:T(8,128)(2,1)S(1)}, u32[]{:S(2)}, u32[]{:S(2)}) async-start(bf16[16,64,128]{2,1,0:T(8,128)(2,1)} %bitcast.7), calls=%async_computation.4 | async-start | bytes 524288 | tf_op jit(solution)/shard_map/all_to_all | solution.py:285
  133.1 6.1 %all-to-all-done.4 = bf16[16,64,128]{2,1,0:T(8,128)(2,1)S(1)} async-done(((bf16[16,64,128]{2,1,0:T(8,128)(2,1)}), bf16[16,64,128]{2,1,0:T(8,128)(2,1)S(1)}, u32[]{:S(2)}, u32[]{:S(2)}) %all-to-all-start.4) | async-done | bytes 262176 | tf_op jit(solution)/shard_map/all_to_all | solution.py:285
  139.3 12.1 %all_to_all.37 = f32[8,72,128]{2,1,0:T(8,128)S(1)} all-to-all(f32[8,72,128]{2,1,0:T(8,128)S(1)} %broadcast_in_dim.13), channel_id=1, replica_groups=mesh['y'=4,'xl'=2,'c'=2,'z'=8,'xh'=2] {'z'}, dimensions={0} | all-to-all | bytes 589824 | tf_op jit(solution)/shard_map/all_to_all | solution.py:261
  151.4 11.6 %all_to_all.38 = bf16[16,64,128]{2,1,0:T(8,128)(2,1)S(1)} all-to-all(bf16[16,64,128]{2,1,0:T(8,128)(2,1)S(1)} %broadcast_in_dim.14), channel_id=1, replica_groups=mesh['y'=4,'xl'=2,'c'=2,'z'=8,'xh'=2] {'y','xl','xh'}, dimensions={0} | all-to-all | bytes 524288 | tf_op jit(solution)/shard_map/all_to_all | solution.py:261
  163.1 4.5 %collective-permute-start.4 = (bf16[1024,128]{1,0:T(8,128)(2,1)S(1)}, bf16[1024,128]{1,0:T(8,128)(2,1)S(1)}, u32[]{:S(2)}, u32[]{:S(2)}) collective-permute-start(bf16[1024,128]{1,0:T(8,128)(2,1)S(1)} %bitcast.16), channel_id=1, source_target_pairs={{0,16},{16,0},{1,17},{17,1},{2,18},{18,2},{3,19},{19,3},{4,20},{20... | collective-permute-start | bytes 786440 | tf_op jit(solution)/shard_map/ppermute | solution.py:256
  168.9 1.0 maximum_convert_fusion
  (27 shorter events, 5.7 us)
Async XLA Ops:
  26.4 19.2 %copy-start.2 = (bf16[8,192,128]{2,1,0:T(8,128)(2,1)}, bf16[8,192,128]{2,1,0:T(8,128)(2,1)S(1)}, u32[]{:S(2)}) copy-start(bf16[8,192,128]{2,1,0:T(8,128)(2,1)S(1)} %all_to_all.35) | copy-start | bytes 1179652
  28.3 17.4 %all-to-all-start.1 = ((bf16[16,192,128]{2,1,0:T(8,128)(2,1)}), bf16[16,192,128]{2,1,0:T(8,128)(2,1)S(1)}, u32[]{:S(2)}, u32[]{:S(2)}) async-start(bf16[16,192,128]{2,1,0:T(8,128)(2,1)} %broadcast_in_dim.11), calls=%async_computation.1 | async-start | bytes 1572864 | tf_op jit(solution)/shard_map/all_to_all | solution.py:261
  35.0 10.6 %collective-permute-start = (bf16[1536,128]{1,0:T(8,128)(2,1)S(1)}, bf16[1536,128]{1,0:T(8,128)(2,1)S(1)}, u32[]{:S(2)}, u32[]{:S(2)}) collective-permute-start(bf16[1536,128]{1,0:T(8,128)(2,1)S(1)} %bitcast.14), channel_id=1, source_target_pairs={{0,16},{16,0},{1,17},{17,1},{2,18},{18,2},{3,19},{19,3},{4,20},{20... | collective-permute-start | bytes 1179656 | tf_op jit(solution)/shard_map/ppermute | solution.py:256
  45.6 0.9 copy-start
  45.6 1.0 copy-start.3
  79.7 10.9 %collective-permute-start.1 = (bf16[1536,256]{1,0:T(8,128)(2,1)}, bf16[1536,256]{1,0:T(8,128)(2,1)S(1)}, u32[]{:S(2)}, u32[]{:S(2)}) collective-permute-start(bf16[1536,256]{1,0:T(8,128)(2,1)} %get-tuple-element.21), channel_id=1, source_target_pairs={{0,16},{16,0},{1,17},{17,1},{2,18},{18,2},{3,19},{19,3},{4,20},{20... | collective-permute-start | bytes 2359304 | tf_op jit(solution)/shard_map/ppermute | solution.py:256
  93.1 27.1 %all-to-all-start.3 = ((bf16[8,192,256]{2,1,0:T(8,128)(2,1)}), bf16[8,192,256]{2,1,0:T(8,128)(2,1)S(1)}, u32[]{:S(2)}, u32[]{:S(2)}) async-start(bf16[8,192,256]{2,1,0:T(8,128)(2,1)} %bitcast.6), calls=%async_computation.3 | async-start | bytes 1572864 | tf_op jit(solution)/shard_map/all_to_all | solution.py:281
  120.2 0.9 copy-start.1
  121.1 10.7 %copy-start.4 = (f32[8,128]{1,0:T(8,128)S(1)}, f32[8,128]{1,0:T(8,128)}, u32[]{:S(2)}) copy-start(f32[8,128]{1,0:T(8,128)} %get-tuple-element.27) | copy-start | bytes 12292
  124.7 1.8 %collective-permute-start.2 = (bf16[1024,128]{1,0:T(8,128)(2,1)}, bf16[1024,128]{1,0:T(8,128)(2,1)S(1)}, u32[]{:S(2)}, u32[]{:S(2)}) collective-permute-start(bf16[1024,128]{1,0:T(8,128)(2,1)} %get-tuple-element.26), channel_id=1, source_target_pairs={{0,16},{16,0},{1,17},{17,1},{2,18},{18,2},{3,19},{19,3},{4,20},{20... | collective-permute-start | bytes 786440 | tf_op jit(solution)/shard_map/ppermute | solution.py:256
  128.3 10.9 %all-to-all-start.4 = ((bf16[16,64,128]{2,1,0:T(8,128)(2,1)}), bf16[16,64,128]{2,1,0:T(8,128)(2,1)S(1)}, u32[]{:S(2)}, u32[]{:S(2)}) async-start(bf16[16,64,128]{2,1,0:T(8,128)(2,1)} %bitcast.7), calls=%async_computation.4 | async-start | bytes 524288 | tf_op jit(solution)/shard_map/all_to_all | solution.py:285
  131.8 1.3 collective-permute-start.3
  163.1 5.7 %collective-permute-start.4 = (bf16[1024,128]{1,0:T(8,128)(2,1)S(1)}, bf16[1024,128]{1,0:T(8,128)(2,1)S(1)}, u32[]{:S(2)}, u32[]{:S(2)}) collective-permute-start(bf16[1024,128]{1,0:T(8,128)(2,1)S(1)} %bitcast.16), channel_id=1, source_target_pairs={{0,16},{16,0},{1,17},{17,1},{2,18},{18,2},{3,19},{19,3},{4,20},{20... | collective-permute-start | bytes 786440 | tf_op jit(solution)/shard_map/ppermute | solution.py:256

commit v2 on v0

v2 whole, which is shorter than its diff:
```python
import jax
import jax.numpy as jnp
from jax import lax
from jax.experimental import pallas as pl
from jax.experimental.pallas import tpu as pltpu
from jax.sharding import Mesh
from jax.sharding import PartitionSpec as P

inverse_tau = 10.0
norm_epsilon = 1e-06
log2_e = 1.4426950408889634

AXES = ("y", "xl", "c", "z", "xh")
PLANE = ("y", "xl", "xh")
COLUMN = ("z", "c")
WIDE = ("y", "xl", "xh", "c")
ROWS = 192
WIDTH = 128
D_IN = 2048
SPAN = 16 * ROWS
TILES = SPAN // WIDTH
SHARE = D_IN // 32
MEBI = 1024 * 1024

VMEM = pl.BlockSpec(memory_space=pltpu.VMEM)
SMEM = pl.BlockSpec(memory_space=pltpu.SMEM)


def params(size):
    return pltpu.CompilerParams(vmem_limit_bytes=size * MEBI)


def total_of(values):
    return jnp.sum(jnp.sum(values, axis=1, keepdims=True), axis=0, keepdims=True)


def project_body(hidden_ref, weight_ref, partner_ref, projected_ref, features_ref, copies_ref, pair_ref, pair_sum_ref):
    projected = jnp.dot(hidden_ref[...], weight_ref[...], preferred_element_type=jnp.float32)
    inverse_norm = lax.rsqrt(jnp.sum(projected * projected, axis=1, keepdims=True) + norm_epsilon)
    features = (projected * inverse_norm).astype(jnp.bfloat16)
    features_ref[...] = features
    for k in range(16):
        copies_ref[k] = features
    places = lax.rem(partner_ref[...], ROWS)
    picks = lax.broadcasted_iota(jnp.int32, (ROWS, ROWS), 0) == places
    paired = jnp.dot(
        jnp.where(picks, 1.0, 0.0).astype(jnp.bfloat16), features, preferred_element_type=jnp.float32
    )
    projected_ref[...] = projected
    pair_ref[...] = paired
    total = total_of(features.astype(jnp.float32) * paired)
    pair_sum_ref[...] = jnp.broadcast_to(inverse_tau * total, (8, WIDTH))


def project(hidden, weight, partner):
    return pl.pallas_call(
        project_body,
        in_specs=[VMEM] * 3,
        out_specs=(VMEM,) * 5,
        out_shape=(
            jax.ShapeDtypeStruct((ROWS, WIDTH), jnp.float32),
            jax.ShapeDtypeStruct((ROWS, WIDTH), jnp.bfloat16),
            pltpu.VMEM((16, ROWS, WIDTH), jnp.bfloat16),
            jax.ShapeDtypeStruct((ROWS, WIDTH), jnp.float32),
            jax.ShapeDtypeStruct((8, WIDTH), jnp.float32),
        ),
        compiler_params=params(8),
        name="project",
    )(hidden, weight, partner.reshape(1, ROWS))


def score_body(place_ref, rows_ref, columns_ref, pair_sum_ref, powers_ref, sums_ref, left, right):
    for b in range(16):
        shard = rows_ref[lax.rem(place_ref[0] + b, 16)]
        scaled = shard.astype(jnp.float32) * (inverse_tau * log2_e)
        high = scaled.astype(jnp.bfloat16)
        left[b * ROWS : (b + 1) * ROWS, :WIDTH] = high
        left[b * ROWS : (b + 1) * ROWS, WIDTH:] = (scaled - high.astype(jnp.float32)).astype(jnp.bfloat16)
    chunk = 2 * WIDTH
    for n in range(SPAN // chunk):
        columns = slice(n * chunk, (n + 1) * chunk)
        piece = jnp.transpose(columns_ref[columns, :])
        right[:WIDTH, columns] = piece
        right[WIDTH:, columns] = piece
    for n in range(SPAN // chunk):
        columns = slice(n * chunk, (n + 1) * chunk)
        powers = jnp.exp2(jnp.dot(left[...], right[:, columns], preferred_element_type=jnp.float32))
        own_row = lax.broadcasted_iota(jnp.int32, (ROWS, chunk), 0) + place_ref[1] * ROWS
        own_column = lax.broadcasted_iota(jnp.int32, (ROWS, chunk), 1) + n * chunk
        first = jnp.where(own_row == own_column, 0.0, powers[:ROWS, :])
        rest = powers[ROWS:, :]
        powers_ref[:ROWS, columns] = first.astype(jnp.bfloat16)
        powers_ref[ROWS:, columns] = rest.astype(jnp.bfloat16)
        sums = jnp.sum(first.reshape(ROWS // 8, 8, chunk), axis=0)
        sums += jnp.sum(rest.reshape((SPAN - ROWS) // 8, 8, chunk), axis=0)
        sums = jnp.sum(sums, axis=0, keepdims=True)
        for half in range(2):
            part = jnp.broadcast_to(sums[:, half * WIDTH : (half + 1) * WIDTH].reshape(1, 1, WIDTH), (16, 1, WIDTH))
            sums_ref[:, 2 * n + half : 2 * n + half + 1, :] = part
    sums_ref[:, TILES:, :] = jnp.broadcast_to(pair_sum_ref[...].reshape(1, 8, WIDTH), (16, 8, WIDTH))


def score(place, rows, columns, pair_sum):
    return pl.pallas_call(
        score_body,
        in_specs=[SMEM] + [VMEM] * 3,
        out_specs=(VMEM, VMEM),
        out_shape=(
            pltpu.VMEM((SPAN, SPAN), jnp.bfloat16),
            pltpu.VMEM((16, TILES + 8, WIDTH), jnp.float32),
        ),
        scratch_shapes=[
            pltpu.VMEM((SPAN, 2 * WIDTH), jnp.bfloat16),
            pltpu.VMEM((2 * WIDTH, SPAN), jnp.bfloat16),
        ],
        compiler_params=params(20),
        name="score",
    )(place, rows, columns, pair_sum)


def weigh_body(place_ref, partial_ref, columns_ref, powers_ref, out_ref, own_ref, loss_ref, inverse, both):
    sums = jnp.sum(partial_ref[...], axis=0)
    totals = sums[:TILES, :]
    loss_ref[...] = total_of(jnp.log(totals)) - sums[TILES:, :]
    inverses = 1.0 / totals
    for k in range(TILES):
        rows = slice(k * WIDTH, (k + 1) * WIDTH)
        turned = jnp.transpose(jnp.broadcast_to(inverses[k : k + 1, :], (WIDTH, WIDTH)))
        inverse[rows, :] = turned
        piece = columns_ref[rows, :]
        both[rows, :WIDTH] = piece
        both[rows, WIDTH:] = (piece.astype(jnp.float32) * turned).astype(jnp.bfloat16)
    own_ref[...] = inverse[pl.ds(pl.multiple_of(place_ref[1] * ROWS, ROWS), ROWS), :]
    block = 4 * ROWS
    for i in range(SPAN // block):
        weighed = jnp.dot(
            powers_ref[i * block : (i + 1) * block, :], both[...], preferred_element_type=jnp.float32
        ).astype(jnp.bfloat16)
        for b in range(4):
            out_ref[lax.rem(place_ref[0] + 4 * i + b, 16)] = weighed[b * ROWS : (b + 1) * ROWS, :]


def weigh(place, partial, columns, powers):
    return pl.pallas_call(
        weigh_body,
        in_specs=[SMEM] + [VMEM] * 3,
        out_specs=(VMEM,) * 3,
        out_shape=(
            pltpu.VMEM((16, ROWS, 2 * WIDTH), jnp.bfloat16),
            jax.ShapeDtypeStruct((ROWS, WIDTH), jnp.float32),
            jax.ShapeDtypeStruct((8, WIDTH), jnp.float32),
        ),
        scratch_shapes=[
            pltpu.VMEM((SPAN, WIDTH), jnp.float32),
            pltpu.VMEM((SPAN, 2 * WIDTH), jnp.bfloat16),
        ],
        compiler_params=params(20),
        name="weigh",
    )(place, partial, columns, powers)


def gradient_body(arrived_ref, inverse_ref, pair_ref, projected_ref, hidden_ref, derivative_ref, grad_ref):
    sums = jnp.sum(arrived_ref[...].astype(jnp.float32), axis=0)
    mixed = inverse_ref[...] * sums[:, :WIDTH] + sums[:, WIDTH:]
    derivative = inverse_tau * (mixed - 2.0 * pair_ref[...])
    derivative_ref[...] = derivative
    projected = projected_ref[...]
    inverse_norm = lax.rsqrt(jnp.sum(projected * projected, axis=1, keepdims=True) + norm_epsilon)
    unit = projected * inverse_norm
    alongside = jnp.sum(unit * derivative, axis=1, keepdims=True)
    projected_grad = ((derivative - unit * alongside) * inverse_norm).astype(jnp.bfloat16)
    grad_ref[...] = lax.dot_general(
        hidden_ref[...], projected_grad, (((0,), (0,)), ((), ())), preferred_element_type=jnp.float32
    ).astype(jnp.bfloat16)


def gradient(arrived, inverse, pair, projected, hidden):
    return pl.pallas_call(
        gradient_body,
        in_specs=[VMEM] * 5,
        out_specs=(VMEM, VMEM),
        out_shape=(
            jax.ShapeDtypeStruct((ROWS, WIDTH), jnp.float32),
            pltpu.VMEM((D_IN, WIDTH), jnp.bfloat16),
        ),
        compiler_params=params(16),
        name="gradient",
    )(arrived, inverse, pair, projected, hidden)


def share_body(arrived_ref, copies_ref):
    total = jnp.sum(arrived_ref[...].astype(jnp.float32), axis=0)
    for k in range(8):
        copies_ref[k] = total


def share(arrived):
    return pl.pallas_call(
        share_body,
        in_specs=[VMEM],
        out_specs=VMEM,
        out_shape=pltpu.VMEM((8, SHARE, WIDTH), jnp.float32),
        compiler_params=params(8),
        name="share",
    )(arrived)


def packet_body(arrived_ref, loss_ref, copies_ref):
    total = jnp.sum(arrived_ref[...], axis=0).astype(jnp.bfloat16)
    loss = jnp.broadcast_to(loss_ref[0:1, :], (16, WIDTH))
    high = loss.astype(jnp.bfloat16).astype(jnp.float32)
    middle = (loss - high).astype(jnp.bfloat16).astype(jnp.float32)
    low = loss - high - middle
    row = lax.broadcasted_iota(jnp.int32, (16, WIDTH), 0)
    pieces = jnp.where(row == 0, high, jnp.where(row == 1, middle, jnp.where(row == 2, low, 0.0)))
    pieces = pieces.astype(jnp.bfloat16)
    for k in range(32):
        copies_ref[k, :SHARE, :] = total
        copies_ref[k, SHARE:, :] = pieces


def packet(arrived, loss):
    return pl.pallas_call(
        packet_body,
        in_specs=[VMEM] * 2,
        out_specs=VMEM,
        out_shape=pltpu.VMEM((32, SHARE + 16, WIDTH), jnp.bfloat16),
        compiler_params=params(8),
        name="packet",
    )(arrived, loss)


def finish_body(arrived_ref, loss_ref, grad_ref):
    for k in range(32):
        grad_ref[k] = arrived_ref[k, :SHARE, :].astype(jnp.float32)
    pieces = jnp.sum(arrived_ref[:, SHARE:, :].astype(jnp.float32), axis=0)
    loss_ref[...] = jnp.sum(pieces[:, 0:1], axis=0, keepdims=True) * (0.5 / (256 * ROWS))


def finish(arrived):
    return pl.pallas_call(
        finish_body,
        in_specs=[VMEM],
        out_specs=(VMEM, VMEM),
        out_shape=(
            jax.ShapeDtypeStruct((1, 1), jnp.float32),
            jax.ShapeDtypeStruct((32, SHARE, WIDTH), jnp.float32),
        ),
        compiler_params=params(8),
        name="finish",
    )(arrived)


def local(hidden, weight, partner):
    plane_place = (lax.axis_index("y") * 2 + lax.axis_index("xl")) * 2 + lax.axis_index("xh")
    column_place = lax.axis_index("z") * 2 + lax.axis_index("c")
    place = jnp.stack([plane_place, column_place]).astype(jnp.int32)

    projected, features, copies, pair, pair_sum = project(hidden, weight, partner)
    columns = lax.all_gather(features, COLUMN, axis=0, tiled=True)
    rows = lax.all_to_all(copies, PLANE, 0, 0)
    powers, sums = score(place, rows, columns, pair_sum)
    partial = lax.all_to_all(sums, COLUMN, 0, 0)
    weighed, inverse, loss = weigh(place, partial, columns, powers)
    arrived = lax.all_to_all(weighed, PLANE, 0, 0)
    derivative, grad = gradient(arrived, inverse, pair, projected, hidden)
    shares = lax.all_to_all(grad.reshape(32, SHARE, WIDTH), WIDE, 0, 0)
    shares = lax.all_to_all(share(shares), "z", 0, 0)
    packets = lax.all_to_all(packet(shares, loss), WIDE, 0, 0)
    mean_loss, grad_weight = finish(packets)
    return (mean_loss.reshape(()), derivative, grad_weight.reshape(D_IN, WIDTH))


def solution(mesh):
    split = Mesh(mesh.devices.reshape(4, 2, 2, 8, 2), AXES)
    return jax.shard_map(
        local,
        mesh=split,
        in_specs=(P(AXES, None), P(), P(AXES)),
        out_specs=(P(), P(AXES, None), P()),
        check_vma=False,
    )
```

time: 607 us -> 142 us (0.23)
  waiting for transfers between devices: 250 us -> 0.01 us
  blocking collectives: 214 us -> 115 us
  matrix products: 76.7 us -> 0 us
  loops' own time: 21.6 us -> 0 us
  local copies, waits for them, and re-layouts: 24.4 us -> 2.85 us
  between operations: 16.6 us -> 0.69 us
  Pallas kernels: 0 us -> 15.5 us
  starting transfers between devices: 0.08 us -> 7.58 us
    psum x1 -> x0, waiting for transfers between devices: 174 us -> none  [local(): lax.psum((local_grad, jnp.sum(normalizer_logarithms - paired_scaled_score...]
    all_to_all x0 -> x5, blocking collectives: none -> 92 us  [the longest x1 28.5 us: local(): arrived = lax.all_to_all(weighed, PLANE, 0, 0)]
    dot_general x34 -> x0, matrix products: 76.7 us -> none  [the longest x16 42.5 us: add_weighted(): jnp.dot(mixing, leftover_entries, preferred_element_type=jnp.float32)]
    all_gather x1 -> x0, waiting for transfers between devices: 75.9 us -> none  [local(): lax.all_gather(group_features, 'grp', axis=0, tiled=True)]
    psum x1 -> x0, blocking collectives: 73 us -> none  [local(): lax.psum((local_grad, jnp.sum(normalizer_logarithms - paired_scaled_score...]
    unnamed x1 -> x0, blocking collectives: 63.3 us -> none
    all_gather x2 -> x1, blocking collectives: 77.3 us -> 22.9 us  [local(): columns = lax.all_gather(features, COLUMN, axis=0, tiled=True)]
    another operation x2 -> x0, loops' own time: 21.6 us -> none  [scan_blocks(): lax.scan(advance, initial, (jnp.arange(block_count, dtype=jnp.int32), sta...]
  transfers between devices with their start and end apart: 2 -> 1, of which waited for: 2 -> 0; matrix products, arithmetic and copies ran while one was open for 0% -> 0% of each run, Pallas kernels for 0% -> 0%
where the time goes in v2:
time: 142 us
  blocking collectives  115 us (81%)
  Pallas kernels  15.5 us (11%)
  starting transfers between devices  7.58 us (5%)
  local copies, waits for them, and re-layouts  2.85 us (2%)
    all_to_all x1, blocking collectives, local(): arrived = lax.all_to_all(weighed, PLANE, 0, 0)  28.5 us
    all_gather x1, blocking collectives, local(): columns = lax.all_gather(features, COLUMN, axis=0, tiled=True)  22.9 us
    all_to_all x1, blocking collectives, local(): packets = lax.all_to_all(packet(shares, loss), WIDE, 0, 0)  16.9 us
    all_to_all x1, blocking collectives, local(): shares = lax.all_to_all(grad.reshape(32, SHARE, WIDTH), WIDE, 0, 0)  16.6 us
    all_to_all x1, blocking collectives, local(): partial = lax.all_to_all(sums, COLUMN, 0, 0)  15.3 us
    all_to_all x1, blocking collectives, local(): shares = lax.all_to_all(share(shares), 'z', 0, 0)  14.8 us
    all_to_all x1, starting transfers between devices, local(): rows = lax.all_to_all(copies, PLANE, 0, 0)  7.58 us
    pallas_call x1, Pallas kernels, score(): pl.pallas_call(score_body, in_specs=[SMEM] + [VMEM] * 3, out_specs=(VMEM,...  6.17 us
  transfers between devices with their start and end apart: 1, of which 0 were waited for; matrix products, arithmetic and copies ran while one was open for 0% of the time, Pallas kernels for 0%

profile of v2, /device:TPU:1, one launch (start us, length us, event | category | flops | bytes accessed | tf_op | source)
XLA Modules:
  0.0 141.6 jit_solution(7838518723452831594)
XLA Ops:
  0.6 0.0 copy-start
  0.6 1.1 copy-done
  1.8 0.0 copy-start.2
  1.8 1.0 copy-done.2
  2.8 0.0 copy-start.3
  2.8 0.7 copy-done.3
  3.5 1.4 project.1
  4.9 7.6 %all-to-all-start = ((bf16[16,192,128]{2,1,0:T(8,128)(2,1)}), bf16[16,192,128]{2,1,0:T(8,128)(2,1)S(1)}, u32[]{:S(2)}, u32[]{:S(2)}) async-start(bf16[16,192,128]{2,1,0:T(8,128)(2,1)} %get-tuple-element.17), calls=%async_computation | async-start | bytes 1572864 | tf_op jit(solution)/shard_map/all_to_all | solution.py:261
  12.5 0.1 pad_add_fusion.place_ref
  12.6 22.9 %all_gather.3.columns_ref = bf16[3072,128]{1,0:T(8,128)(2,1)S(1)} all-gather(bf16[192,128]{1,0:T(8,128)(2,1)S(1)} %get-tuple-element.18), channel_id=1, replica_groups=mesh['y'=4,'xl'=2,'c'=2,'z'=8,'xh'=2] {'z','c'}, dimensions={0}, use_global_device_ids=true | all-gather | bytes 835584 | tf_op jit(solution)/shard_map/all_gather | solution.py:260
  35.5 0.0 all-to-all-done.rows_ref
  35.5 6.2 %score.1 = (bf16[3072,3072]{1,0:T(8,128)(2,1)S(1)}, f32[16,32,128]{2,1,0:T(8,128)S(1)}) custom-call(s32[2]{0:T(128)S(1)} %pad_add_fusion.place_ref, bf16[16,192,128]{2,1,0:T(8,128)(2,1)S(1)} %all-to-all-done.rows_ref, bf16[3072,128]{1,0:T(8,128)(2,1)S(1)} %all_gather.3.columns_ref, f32[8,128]{1,0:T(8,128)S(1)} %get-tuple-element.19.pair_sum_ref), custom_call_target="tpu_custom_call" | custom-call | tf_op jit(solution)/shard_map/score/pallas_call | solution.py:104
  41.6 15.3 %all_to_all.30.partial_ref = f32[16,32,128]{2,1,0:T(8,128)S(1)} all-to-all(f32[16,32,128]{2,1,0:T(8,128)S(1)} %get-tuple-element.20), channel_id=1, replica_groups=mesh['y'=4,'xl'=2,'c'=2,'z'=8,'xh'=2] {'z','c'}, dimensions={0} | all-to-all | bytes 524288 | tf_op jit(solution)/shard_map/all_to_all | solution.py:263
  56.9 5.8 %weigh.1 = (bf16[16,192,256]{2,1,0:T(8,128)(2,1)S(1)}, f32[192,128]{1,0:T(8,128)S(1)}, f32[8,128]{1,0:T(8,128)S(1)}) custom-call(s32[2]{0:T(128)S(1)} %pad_add_fusion.place_ref, f32[16,32,128]{2,1,0:T(8,128)S(1)} %all_to_all.30.partial_ref, bf16[3072,128]{1,0:T(8,128)(2,1)S(1)} %all_gather.3.columns_ref, bf16[3072,3072]{1,0:T(8,128)(2,1)S(1)} %get-tuple-element.21.powers_ref), custom_call_target="tpu_custom_call" | custom-call | tf_op jit(solution)/shard_map/weigh/pallas_call | solution.py:144
  62.7 0.0 copy-start.1
  62.8 28.5 %all_to_all.31.arrived_ref = bf16[16,192,256]{2,1,0:T(8,128)(2,1)S(1)} all-to-all(bf16[16,192,256]{2,1,0:T(8,128)(2,1)S(1)} %get-tuple-element.22), channel_id=1, replica_groups=mesh['y'=4,'xl'=2,'c'=2,'z'=8,'xh'=2] {'y','xl','xh'}, dimensions={0} | all-to-all | bytes 3145728 | tf_op jit(solution)/shard_map/all_to_all | solution.py:265
  91.2 0.0 copy-done.1
  91.2 0.9 gradient.1
  92.1 16.6 %all_to_all.32.arrived_ref = bf16[32,64,128]{2,1,0:T(8,128)(2,1)S(1)} all-to-all(bf16[32,64,128]{2,1,0:T(8,128)(2,1)S(1)} %bitcast.6), channel_id=1, replica_groups=mesh['y'=4,'xl'=2,'c'=2,'z'=8,'xh'=2] {'y','xl','xh','c'}, dimensions={0} | all-to-all | bytes 1048576 | tf_op jit(solution)/shard_map/all_to_all | solution.py:267
  108.7 0.1 share.1
  108.8 14.8 %all_to_all.33.arrived_ref = f32[8,64,128]{2,1,0:T(8,128)S(1)} all-to-all(f32[8,64,128]{2,1,0:T(8,128)S(1)} %share.1), channel_id=1, replica_groups=mesh['y'=4,'xl'=2,'c'=2,'z'=8,'xh'=2] {'z'}, dimensions={0} | all-to-all | bytes 524288 | tf_op jit(solution)/shard_map/all_to_all | solution.py:268
  123.6 0.1 packet.1
  123.6 16.9 %all_to_all.34.arrived_ref = bf16[32,80,128]{2,1,0:T(8,128)(2,1)S(1)} all-to-all(bf16[32,80,128]{2,1,0:T(8,128)(2,1)S(1)} %packet.1), channel_id=1, replica_groups=mesh['y'=4,'xl'=2,'c'=2,'z'=8,'xh'=2] {'y','xl','xh','c'}, dimensions={0} | all-to-all | bytes 1310720 | tf_op jit(solution)/shard_map/all_to_all | solution.py:269
  140.5 1.0 finish.1
Async XLA Ops:
  0.6 1.1 copy-start
  1.8 1.0 copy-start.2
  2.8 0.7 copy-start.3
  4.9 30.6 %all-to-all-start = ((bf16[16,192,128]{2,1,0:T(8,128)(2,1)}), bf16[16,192,128]{2,1,0:T(8,128)(2,1)S(1)}, u32[]{:S(2)}, u32[]{:S(2)}) async-start(bf16[16,192,128]{2,1,0:T(8,128)(2,1)} %get-tuple-element.17), calls=%async_computation | async-start | bytes 1572864 | tf_op jit(solution)/shard_map/all_to_all | solution.py:261
  62.7 28.5 %copy-start.1 = (bf16[192,2048]{1,0:T(8,128)(2,1)S(1)}, bf16[192,2048]{1,0:T(8,128)(2,1)}, u32[]{:S(2)}) copy-start(bf16[192,2048]{1,0:T(8,128)(2,1)} %hidden_ref.3) | copy-start | bytes 2359300

commit v3 on v2

--- a/solution.py
+++ b/solution.py
@@ -13,17 +13,19 @@
 AXES = ("y", "xl", "c", "z", "xh")
 PLANE = ("y", "xl", "xh")
 COLUMN = ("z", "c")
-WIDE = ("y", "xl", "xh", "c")
 ROWS = 192
 WIDTH = 128
 D_IN = 2048
 SPAN = 16 * ROWS
 TILES = SPAN // WIDTH
 SHARE = D_IN // 32
+HALF = D_IN // 2
+PIECES = 2
 MEBI = 1024 * 1024
 
 VMEM = pl.BlockSpec(memory_space=pltpu.VMEM)
 SMEM = pl.BlockSpec(memory_space=pltpu.SMEM)
+ANY = pl.BlockSpec(memory_space=pl.ANY)
 
 
 def params(size):
@@ -34,14 +36,38 @@
     return jnp.sum(jnp.sum(values, axis=1, keepdims=True), axis=0, keepdims=True)
 
 
-def project_body(hidden_ref, weight_ref, partner_ref, projected_ref, features_ref, copies_ref, pair_ref, pair_sum_ref):
-    projected = jnp.dot(hidden_ref[...], weight_ref[...], preferred_element_type=jnp.float32)
+def project_body(
+    hidden_hbm, weight_hbm, partner_hbm, projected_ref, features_ref, copies_ref, pair_ref, pair_sum_ref,
+    hidden, weight, partner, hidden_done, weight_done, partner_done,
+):
+    depth = D_IN // PIECES
+    copies = []
+    for k in range(PIECES):
+        part = slice(k * depth, (k + 1) * depth)
+        copies.append(
+            (
+                pltpu.make_async_copy(hidden_hbm.at[:, part], hidden.at[:, part], hidden_done.at[k]),
+                pltpu.make_async_copy(weight_hbm.at[part, :], weight.at[part, :], weight_done.at[k]),
+            )
+        )
+    partner_copy = pltpu.make_async_copy(partner_hbm, partner, partner_done)
+    for first, second in copies:
+        first.start()
+        second.start()
+    partner_copy.start()
+    projected = jnp.zeros((ROWS, WIDTH), jnp.float32)
+    for k in range(PIECES):
+        part = slice(k * depth, (k + 1) * depth)
+        for copy in copies[k]:
+            copy.wait()
+        projected += jnp.dot(hidden[:, part], weight[part, :], preferred_element_type=jnp.float32)
     inverse_norm = lax.rsqrt(jnp.sum(projected * projected, axis=1, keepdims=True) + norm_epsilon)
     features = (projected * inverse_norm).astype(jnp.bfloat16)
     features_ref[...] = features
     for k in range(16):
         copies_ref[k] = features
-    places = lax.rem(partner_ref[...], ROWS)
+    partner_copy.wait()
+    places = lax.rem(partner[...], ROWS)
     picks = lax.broadcasted_iota(jnp.int32, (ROWS, ROWS), 0) == places
     paired = jnp.dot(
         jnp.where(picks, 1.0, 0.0).astype(jnp.bfloat16), features, preferred_element_type=jnp.float32
@@ -55,7 +81,7 @@
 def project(hidden, weight, partner):
     return pl.pallas_call(
         project_body,
-        in_specs=[VMEM] * 3,
+        in_specs=[ANY] * 3,
         out_specs=(VMEM,) * 5,
         out_shape=(
             jax.ShapeDtypeStruct((ROWS, WIDTH), jnp.float32),
@@ -64,6 +90,14 @@
             jax.ShapeDtypeStruct((ROWS, WIDTH), jnp.float32),
             jax.ShapeDtypeStruct((8, WIDTH), jnp.float32),
         ),
+        scratch_shapes=[
+            pltpu.VMEM((ROWS, D_IN), jnp.bfloat16),
+            pltpu.VMEM((D_IN, WIDTH), jnp.bfloat16),
+            pltpu.VMEM((1, ROWS), jnp.int32),
+            pltpu.SemaphoreType.DMA((PIECES,)),
+            pltpu.SemaphoreType.DMA((PIECES,)),
+            pltpu.SemaphoreType.DMA,
+        ],
         compiler_params=params(8),
         name="project",
     )(hidden, weight, partner.reshape(1, ROWS))
@@ -95,9 +129,8 @@
         sums += jnp.sum(rest.reshape((SPAN - ROWS) // 8, 8, chunk), axis=0)
         sums = jnp.sum(sums, axis=0, keepdims=True)
         for half in range(2):
-            part = jnp.broadcast_to(sums[:, half * WIDTH : (half + 1) * WIDTH].reshape(1, 1, WIDTH), (16, 1, WIDTH))
-            sums_ref[:, 2 * n + half : 2 * n + half + 1, :] = part
-    sums_ref[:, TILES:, :] = jnp.broadcast_to(pair_sum_ref[...].reshape(1, 8, WIDTH), (16, 8, WIDTH))
+            sums_ref[2 * n + half : 2 * n + half + 1, :] = sums[:, half * WIDTH : (half + 1) * WIDTH]
+    sums_ref[TILES:, :] = pair_sum_ref[...]
 
 
 def score(place, rows, columns, pair_sum):
@@ -107,7 +140,7 @@
         out_specs=(VMEM, VMEM),
         out_shape=(
             pltpu.VMEM((SPAN, SPAN), jnp.bfloat16),
-            pltpu.VMEM((16, TILES + 8, WIDTH), jnp.float32),
+            pltpu.VMEM((TILES + 8, WIDTH), jnp.float32),
         ),
         scratch_shapes=[
             pltpu.VMEM((SPAN, 2 * WIDTH), jnp.bfloat16),
@@ -116,6 +149,23 @@
         compiler_params=params(20),
         name="score",
     )(place, rows, columns, pair_sum)
+
+
+def spread_body(arrived_ref, copies_ref):
+    total = arrived_ref[: TILES + 8, :] + arrived_ref[TILES + 8 :, :]
+    for k in range(8):
+        copies_ref[k] = total
+
+
+def spread(arrived):
+    return pl.pallas_call(
+        spread_body,
+        in_specs=[VMEM],
+        out_specs=VMEM,
+        out_shape=pltpu.VMEM((8, TILES + 8, WIDTH), jnp.float32),
+        compiler_params=params(4),
+        name="spread",
+    )(arrived)
 
 
 def weigh_body(place_ref, partial_ref, columns_ref, powers_ref, out_ref, own_ref, loss_ref, inverse, both):
@@ -159,7 +209,9 @@
     )(place, partial, columns, powers)
 
 
-def gradient_body(arrived_ref, inverse_ref, pair_ref, projected_ref, hidden_ref, derivative_ref, grad_ref):
+def gradient_body(
+    core_ref, arrived_ref, inverse_ref, pair_ref, projected_ref, hidden_ref, derivative_ref, own_ref, other_ref
+):
     sums = jnp.sum(arrived_ref[...].astype(jnp.float32), axis=0)
     mixed = inverse_ref[...] * sums[:, :WIDTH] + sums[:, WIDTH:]
     derivative = inverse_tau * (mixed - 2.0 * pair_ref[...])
@@ -169,27 +221,51 @@
     unit = projected * inverse_norm
     alongside = jnp.sum(unit * derivative, axis=1, keepdims=True)
     projected_grad = ((derivative - unit * alongside) * inverse_norm).astype(jnp.bfloat16)
-    grad_ref[...] = lax.dot_general(
-        hidden_ref[...], projected_grad, (((0,), (0,)), ((), ())), preferred_element_type=jnp.float32
-    ).astype(jnp.bfloat16)
-
-
-def gradient(arrived, inverse, pair, projected, hidden):
+
+    def product(half):
+        columns = pl.ds(pl.multiple_of(half * HALF, HALF), HALF)
+        return lax.dot_general(
+            hidden_ref[:, columns], projected_grad, (((0,), (0,)), ((), ())), preferred_element_type=jnp.float32
+        )
+
+    own_ref[...] = product(core_ref[0])
+    other_ref[...] = product(1 - core_ref[0]).astype(jnp.bfloat16)
+
+
+def gradient(core, arrived, inverse, pair, projected, hidden):
     return pl.pallas_call(
         gradient_body,
-        in_specs=[VMEM] * 5,
-        out_specs=(VMEM, VMEM),
+        in_specs=[SMEM] + [VMEM] * 5,
+        out_specs=(VMEM,) * 3,
         out_shape=(
             jax.ShapeDtypeStruct((ROWS, WIDTH), jnp.float32),
-            pltpu.VMEM((D_IN, WIDTH), jnp.bfloat16),
+            pltpu.VMEM((HALF, WIDTH), jnp.float32),
+            pltpu.VMEM((HALF, WIDTH), jnp.bfloat16),
         ),
         compiler_params=params(16),
         name="gradient",
-    )(arrived, inverse, pair, projected, hidden)
+    )(core, arrived, inverse, pair, projected, hidden)
+
+
+def join_body(own_ref, other_ref, sum_ref):
+    for k in range(16):
+        part = slice(k * SHARE, (k + 1) * SHARE)
+        sum_ref[k] = (own_ref[part, :] + other_ref[part, :].astype(jnp.float32)).astype(jnp.bfloat16)
+
+
+def join(own, other):
+    return pl.pallas_call(
+        join_body,
+        in_specs=[VMEM] * 2,
+        out_specs=VMEM,
+        out_shape=pltpu.VMEM((16, SHARE, WIDTH), jnp.bfloat16),
+        compiler_params=params(4),
+        name="join",
+    )(own, other)
 
 
 def share_body(arrived_ref, copies_ref):
-    total = jnp.sum(arrived_ref[...].astype(jnp.float32), axis=0)
+    total = jnp.sum(arrived_ref[...].astype(jnp.float32), axis=0).astype(jnp.bfloat16)
     for k in range(8):
         copies_ref[k] = total
 
@@ -199,14 +275,14 @@
         share_body,
         in_specs=[VMEM],
         out_specs=VMEM,
-        out_shape=pltpu.VMEM((8, SHARE, WIDTH), jnp.float32),
-        compiler_params=params(8),
+        out_shape=pltpu.VMEM((8, SHARE, WIDTH), jnp.bfloat16),
+        compiler_params=params(4),
         name="share",
     )(arrived)
 
 
 def packet_body(arrived_ref, loss_ref, copies_ref):
-    total = jnp.sum(arrived_ref[...], axis=0).astype(jnp.bfloat16)
+    total = jnp.sum(arrived_ref[...].astype(jnp.float32), axis=0).astype(jnp.bfloat16)
     loss = jnp.broadcast_to(loss_ref[0:1, :], (16, WIDTH))
     high = loss.astype(jnp.bfloat16).astype(jnp.float32)
     middle = (loss - high).astype(jnp.bfloat16).astype(jnp.float32)
@@ -214,7 +290,7 @@
     row = lax.broadcasted_iota(jnp.int32, (16, WIDTH), 0)
     pieces = jnp.where(row == 0, high, jnp.where(row == 1, middle, jnp.where(row == 2, low, 0.0)))
     pieces = pieces.astype(jnp.bfloat16)
-    for k in range(32):
+    for k in range(16):
         copies_ref[k, :SHARE, :] = total
         copies_ref[k, SHARE:, :] = pieces
 
@@ -224,7 +300,7 @@
         packet_body,
         in_specs=[VMEM] * 2,
         out_specs=VMEM,
-        out_shape=pltpu.VMEM((32, SHARE + 16, WIDTH), jnp.bfloat16),
+        out_shape=pltpu.VMEM((16, SHARE + 16, WIDTH), jnp.bfloat16),
         compiler_params=params(8),
         name="packet",
     )(arrived, loss)
@@ -254,19 +330,23 @@
 def local(hidden, weight, partner):
     plane_place = (lax.axis_index("y") * 2 + lax.axis_index("xl")) * 2 + lax.axis_index("xh")
     column_place = lax.axis_index("z") * 2 + lax.axis_index("c")
+    core = lax.axis_index("c").astype(jnp.int32).reshape(1)
     place = jnp.stack([plane_place, column_place]).astype(jnp.int32)
 
     projected, features, copies, pair, pair_sum = project(hidden, weight, partner)
     columns = lax.all_gather(features, COLUMN, axis=0, tiled=True)
     rows = lax.all_to_all(copies, PLANE, 0, 0)
     powers, sums = score(place, rows, columns, pair_sum)
-    partial = lax.all_to_all(sums, COLUMN, 0, 0)
+    sums = spread(lax.all_gather(sums, "c", axis=0, tiled=True))
+    partial = lax.all_to_all(sums, "z", 0, 0)
     weighed, inverse, loss = weigh(place, partial, columns, powers)
     arrived = lax.all_to_all(weighed, PLANE, 0, 0)
-    derivative, grad = gradient(arrived, inverse, pair, projected, hidden)
-    shares = lax.all_to_all(grad.reshape(32, SHARE, WIDTH), WIDE, 0, 0)
+    derivative, own, other = gradient(core, arrived, inverse, pair, projected, hidden)
+    other = lax.ppermute(other, "c", [(0, 1), (1, 0)])
+    shares = lax.all_to_all(join(own, other), PLANE, 0, 0)
     shares = lax.all_to_all(share(shares), "z", 0, 0)
-    packets = lax.all_to_all(packet(shares, loss), WIDE, 0, 0)
+    packets = lax.all_to_all(packet(shares, loss), PLANE, 0, 0)
+    packets = lax.all_gather(packets, "c", axis=0, tiled=True)
     mean_loss, grad_weight = finish(packets)
     return (mean_loss.reshape(()), derivative, grad_weight.reshape(D_IN, WIDTH))
 

time: 142 us -> 133 us (0.937)
  blocking collectives: 115 us -> 100 us
  starting transfers between devices: 7.58 us -> 11.4 us
    all_to_all x3, blocking collectives: 48.7 us -> 32.8 us  [the longest x1 11.5 us: local(): partial = lax.all_to_all(sums, 'z', 0, 0)]
    all_gather x0 -> x2, blocking collectives: none -> 7.97 us  [the longest x1 6.14 us: local(): packets = lax.all_gather(packets, 'c', axis=0, tiled=True)]
    all_to_all x1, blocking collectives: 14.8 us -> 10.4 us  [local(): shares = lax.all_to_all(share(shares), 'z', 0, 0)]
    ppermute x0 -> x1, starting transfers between devices: none -> 3.82 us  [local(): other = lax.ppermute(other, 'c', [(0, 1), (1, 0)])]
    all_to_all x1, blocking collectives: 28.5 us -> 26.3 us  [local(): arrived = lax.all_to_all(weighed, PLANE, 0, 0)]
  transfers between devices with their start and end apart: 1 -> 2, of which waited for: 0 -> 1; matrix products, arithmetic and copies ran while one was open for 0% -> 0% of each run, Pallas kernels for 0% -> 0%
where the time goes in v3:
time: 133 us; the launch traced here: 132 us
  blocking collectives  100 us (75%)
  Pallas kernels  15.4 us (12%)
  starting transfers between devices  11.4 us (9%)
  local copies, waits for them, and re-layouts  2.85 us (2%)
    all_to_all x1, blocking collectives, local(): arrived = lax.all_to_all(weighed, PLANE, 0, 0)  26.3 us
    all_gather x1, blocking collectives, local(): columns = lax.all_gather(features, COLUMN, axis=0, tiled=True)  22.9 us
    all_to_all x1, blocking collectives, local(): partial = lax.all_to_all(sums, 'z', 0, 0)  11.5 us
    all_to_all x1, blocking collectives, local(): packets = lax.all_to_all(packet(shares, loss), PLANE, 0, 0)  10.8 us
    all_to_all x1, blocking collectives, local(): shares = lax.all_to_all(join(own, other), PLANE, 0, 0)  10.5 us
    all_to_all x1, blocking collectives, local(): shares = lax.all_to_all(share(shares), 'z', 0, 0)  10.4 us
    all_to_all x1, starting transfers between devices, local(): rows = lax.all_to_all(copies, PLANE, 0, 0)  7.6 us
    all_gather x1, blocking collectives, local(): packets = lax.all_gather(packets, 'c', axis=0, tiled=True)  6.14 us
  transfers between devices with their start and end apart: 2, of which 1 were waited for; matrix products, arithmetic and copies ran while one was open for 0% of the time, Pallas kernels for 0%

profile of v3, /device:TPU:1, one launch (start us, length us, event | category | flops | bytes accessed | tf_op | source)
XLA Modules:
  0.0 132.1 jit_solution(13722223868900760565)
XLA Ops:
  0.6 0.0 copy-start
  0.6 1.1 copy-done
  1.8 1.0 copy-done.2
  2.8 0.7 copy-done.3
  3.5 1.6 %project.1 = (f32[192,128]{1,0:T(8,128)S(1)}, bf16[192,128]{1,0:T(8,128)(2,1)S(1)}, bf16[16,192,128]{2,1,0:T(8,128)(2,1)}, f32[192,128]{1,0:T(8,128)S(1)}, f32[8,128]{1,0:T(8,128)S(1)}) custom-call(bf16[192,2048]{1,0:T(8,128)(2,1)S(1)} %copy-done, bf16[2048,128]{1,0:T(8,128)(2,1)S(1)} %copy-done.2, s32[1,192]{1,0:T(1,128)S(1)} %bitcast.6), custom_call_target="tpu_custom_call" | custom-call | tf_op jit(solution)/shard_map/project/pallas_call | solution.py:82
  5.1 7.6 %all-to-all-start = ((bf16[16,192,128]{2,1,0:T(8,128)(2,1)}), bf16[16,192,128]{2,1,0:T(8,128)(2,1)S(1)}, u32[]{:S(2)}, u32[]{:S(2)}) async-start(bf16[16,192,128]{2,1,0:T(8,128)(2,1)} %get-tuple-element.18), calls=%async_computation | async-start | bytes 1572864 | tf_op jit(solution)/shard_map/all_to_all | solution.py:338
  12.7 0.1 pad_add_fusion.place_ref
  12.8 22.9 %all_gather.9.columns_ref = bf16[3072,128]{1,0:T(8,128)(2,1)S(1)} all-gather(bf16[192,128]{1,0:T(8,128)(2,1)S(1)} %get-tuple-element.19), channel_id=1, replica_groups=mesh['y'=4,'xl'=2,'c'=2,'z'=8,'xh'=2] {'z','c'}, dimensions={0}, use_global_device_ids=true | all-gather | bytes 835584 | tf_op jit(solution)/shard_map/all_gather | solution.py:337
  35.7 0.0 all-to-all-done.rows_ref
  35.7 5.9 %score.1 = (bf16[3072,3072]{1,0:T(8,128)(2,1)S(1)}, f32[32,128]{1,0:T(8,128)S(1)}) custom-call(s32[2]{0:T(128)S(1)} %pad_add_fusion.place_ref, bf16[16,192,128]{2,1,0:T(8,128)(2,1)S(1)} %all-to-all-done.rows_ref, bf16[3072,128]{1,0:T(8,128)(2,1)S(1)} %all_gather.9.columns_ref, f32[8,128]{1,0:T(8,128)S(1)} %get-tuple-element.20.pair_sum_ref), custom_call_target="tpu_custom_call" | custom-call | tf_op jit(solution)/shard_map/score/pallas_call | solution.py:137
  41.7 1.8 %all_gather.10.arrived_ref = f32[64,128]{1,0:T(8,128)S(1)} all-gather(f32[32,128]{1,0:T(8,128)S(1)} %get-tuple-element.21), channel_id=1, replica_groups=mesh['y'=4,'xl'=2,'c'=2,'z'=8,'xh'=2] {'c'}, dimensions={0}, use_global_device_ids=true | all-gather | bytes 49152 | tf_op jit(solution)/shard_map/all_gather | solution.py:340
  43.5 11.5 %all_to_all.30.partial_ref = f32[8,32,128]{2,1,0:T(8,128)S(1)} all-to-all(f32[8,32,128]{2,1,0:T(8,128)S(1)} %spread.1), channel_id=1, replica_groups=mesh['y'=4,'xl'=2,'c'=2,'z'=8,'xh'=2] {'z'}, dimensions={0} | all-to-all | bytes 262144 | tf_op jit(solution)/shard_map/all_to_all | solution.py:341
  55.0 5.8 %weigh.1 = (bf16[16,192,256]{2,1,0:T(8,128)(2,1)S(1)}, f32[192,128]{1,0:T(8,128)S(1)}, f32[8,128]{1,0:T(8,128)S(1)}) custom-call(s32[2]{0:T(128)S(1)} %pad_add_fusion.place_ref, f32[8,32,128]{2,1,0:T(8,128)S(1)} %all_to_all.30.partial_ref, bf16[3072,128]{1,0:T(8,128)(2,1)S(1)} %all_gather.9.columns_ref, bf16[3072,3072]{1,0:T(8,128)(2,1)S(1)} %get-tuple-element.22.powers_ref), custom_call_target="tpu_custom_call" | custom-call | tf_op jit(solution)/shard_map/weigh/pallas_call | solution.py:194
  60.8 0.0 copy-start.1
  60.8 26.3 %all_to_all.31.arrived_ref = bf16[16,192,256]{2,1,0:T(8,128)(2,1)S(1)} all-to-all(bf16[16,192,256]{2,1,0:T(8,128)(2,1)S(1)} %get-tuple-element.23), channel_id=1, replica_groups=mesh['y'=4,'xl'=2,'c'=2,'z'=8,'xh'=2] {'y','xl','xh'}, dimensions={0} | all-to-all | bytes 3145728 | tf_op jit(solution)/shard_map/all_to_all | solution.py:343
  87.2 0.9 gradient.1
  88.1 3.8 %collective-permute-start = (bf16[1024,128]{1,0:T(8,128)(2,1)S(1)}, bf16[1024,128]{1,0:T(8,128)(2,1)S(1)}, u32[]{:S(2)}, u32[]{:S(2)}) collective-permute-start(bf16[1024,128]{1,0:T(8,128)(2,1)S(1)} %get-tuple-element.28), channel_id=1, source_target_pairs={{0,16},{16,0},{1,17},{17,1},{2,18},{18,2},{3,19},{19,3},{4,20},{20... | collective-permute-start | bytes 786440 | tf_op jit(solution)/shard_map/ppermute | solution.py:345
  91.9 1.2 collective-permute-done.other_ref
  93.0 0.1 join.1
  93.1 10.5 %all_to_all.32.arrived_ref = bf16[16,64,128]{2,1,0:T(8,128)(2,1)S(1)} all-to-all(bf16[16,64,128]{2,1,0:T(8,128)(2,1)S(1)} %join.1), channel_id=1, replica_groups=mesh['y'=4,'xl'=2,'c'=2,'z'=8,'xh'=2] {'y','xl','xh'}, dimensions={0} | all-to-all | bytes 524288 | tf_op jit(solution)/shard_map/all_to_all | solution.py:346
  103.6 10.4 %all_to_all.33.arrived_ref = bf16[8,64,128]{2,1,0:T(8,128)(2,1)S(1)} all-to-all(bf16[8,64,128]{2,1,0:T(8,128)(2,1)S(1)} %share.1), channel_id=1, replica_groups=mesh['y'=4,'xl'=2,'c'=2,'z'=8,'xh'=2] {'z'}, dimensions={0} | all-to-all | bytes 262144 | tf_op jit(solution)/shard_map/all_to_all | solution.py:347
  114.1 10.8 %all_to_all.34 = bf16[16,80,128]{2,1,0:T(8,128)(2,1)S(1)} all-to-all(bf16[16,80,128]{2,1,0:T(8,128)(2,1)S(1)} %packet.1), channel_id=1, replica_groups=mesh['y'=4,'xl'=2,'c'=2,'z'=8,'xh'=2] {'y','xl','xh'}, dimensions={0} | all-to-all | bytes 655360 | tf_op jit(solution)/shard_map/all_to_all | solution.py:348
  124.9 6.1 %all_gather.11.arrived_ref = bf16[32,80,128]{2,1,0:T(8,128)(2,1)S(1)} all-gather(bf16[16,80,128]{2,1,0:T(8,128)(2,1)S(1)} %all_to_all.34), channel_id=1, replica_groups=mesh['y'=4,'xl'=2,'c'=2,'z'=8,'xh'=2] {'c'}, dimensions={0}, use_global_device_ids=true | all-gather | bytes 983040 | tf_op jit(solution)/shard_map/all_gather | solution.py:349
  131.0 1.0 finish.1
  (6 shorter events, 0.1 us)
Async XLA Ops:
  0.6 1.1 copy-start
  1.8 1.0 copy-start.2
  2.8 0.7 copy-start.3
  5.1 30.6 %all-to-all-start = ((bf16[16,192,128]{2,1,0:T(8,128)(2,1)}), bf16[16,192,128]{2,1,0:T(8,128)(2,1)S(1)}, u32[]{:S(2)}, u32[]{:S(2)}) async-start(bf16[16,192,128]{2,1,0:T(8,128)(2,1)} %get-tuple-element.18), calls=%async_computation | async-start | bytes 1572864 | tf_op jit(solution)/shard_map/all_to_all | solution.py:338
  60.8 26.4 %copy-start.1 = (bf16[192,2048]{1,0:T(8,128)(2,1)S(1)}, bf16[192,2048]{1,0:T(8,128)(2,1)}, u32[]{:S(2)}) copy-start(bf16[192,2048]{1,0:T(8,128)(2,1)} %hidden_ref.1) | copy-start | bytes 2359300
  88.1 5.0 %collective-permute-start = (bf16[1024,128]{1,0:T(8,128)(2,1)S(1)}, bf16[1024,128]{1,0:T(8,128)(2,1)S(1)}, u32[]{:S(2)}, u32[]{:S(2)}) collective-permute-start(bf16[1024,128]{1,0:T(8,128)(2,1)S(1)} %get-tuple-element.28), channel_id=1, source_target_pairs={{0,16},{16,0},{1,17},{17,1},{2,18},{18,2},{3,19},{19,3},{4,20},{20... | collective-permute-start | bytes 786440 | tf_op jit(solution)/shard_map/ppermute | solution.py:345

commit v4 on v3

--- a/solution.py
+++ b/solution.py
@@ -98,7 +98,7 @@
             pltpu.SemaphoreType.DMA((PIECES,)),
             pltpu.SemaphoreType.DMA,
         ],
-        compiler_params=params(8),
+        compiler_params=params(60),
         name="project",
     )(hidden, weight, partner.reshape(1, ROWS))
 

time: 133 us -> 131 us (0.985)
  local copies, waits for them, and re-layouts: 2.85 us -> 0.03 us
    unnamed x8 -> x10, local copies, waits for them, and re-layouts: 2.85 us -> 0.03 us
where the time goes in v4:
time: 131 us; the launch traced here: 130 us
  blocking collectives  100 us (76%)
  Pallas kernels  16.6 us (13%)
  starting transfers between devices  11.4 us (9%)
    all_to_all x1, blocking collectives, local(): arrived = lax.all_to_all(weighed, PLANE, 0, 0)  26.3 us
    all_gather x1, blocking collectives, local(): columns = lax.all_gather(features, COLUMN, axis=0, tiled=True)  22.9 us
    all_to_all x1, blocking collectives, local(): partial = lax.all_to_all(sums, 'z', 0, 0)  11.5 us
    all_to_all x1, blocking collectives, local(): packets = lax.all_to_all(packet(shares, loss), PLANE, 0, 0)  10.8 us
    all_to_all x1, blocking collectives, local(): shares = lax.all_to_all(join(own, other), PLANE, 0, 0)  10.5 us
    all_to_all x1, blocking collectives, local(): shares = lax.all_to_all(share(shares), 'z', 0, 0)  10.4 us
    all_to_all x1, starting transfers between devices, local(): rows = lax.all_to_all(copies, PLANE, 0, 0)  7.6 us
    all_gather x1, blocking collectives, local(): packets = lax.all_gather(packets, 'c', axis=0, tiled=True)  6.14 us
  transfers between devices with their start and end apart: 2, of which 1 were waited for; matrix products, arithmetic and copies ran while one was open for 0% of the time, Pallas kernels for 0%

profile of v4, /device:TPU:1, one launch (start us, length us, event | category | flops | bytes accessed | tf_op | source)
XLA Modules:
  0.0 130.4 jit_solution(11053113139698244703)
XLA Ops:
  0.6 2.8 %project.1 = (f32[192,128]{1,0:T(8,128)}, bf16[192,128]{1,0:T(8,128)(2,1)}, bf16[16,192,128]{2,1,0:T(8,128)(2,1)}, f32[192,128]{1,0:T(8,128)}, f32[8,128]{1,0:T(8,128)}) custom-call(bf16[192,2048]{1,0:T(8,128)(2,1)} %hidden_ref.1, bf16[2048,128]{1,0:T(8,128)(2,1)} %weight_hbm.1, s32[1,192]{1,0:T(1,128)} %bitcast.6), custom_call_target="tpu_custom_call" | custom-call | tf_op jit(solution)/shard_map/project/pallas_call | solution.py:82
  3.4 0.0 copy-start.4
  3.4 0.0 copy-start.3
  3.4 7.6 %all-to-all-start = ((bf16[16,192,128]{2,1,0:T(8,128)(2,1)}), bf16[16,192,128]{2,1,0:T(8,128)(2,1)S(1)}, u32[]{:S(2)}, u32[]{:S(2)}) async-start(bf16[16,192,128]{2,1,0:T(8,128)(2,1)} %get-tuple-element.18), calls=%async_computation | async-start | bytes 1572864 | tf_op jit(solution)/shard_map/all_to_all | solution.py:338
  11.0 0.1 pad_add_fusion.place_ref
  11.1 0.0 copy-done.4
  11.1 22.9 %all_gather.9.columns_ref = bf16[3072,128]{1,0:T(8,128)(2,1)S(1)} all-gather(bf16[192,128]{1,0:T(8,128)(2,1)S(1)} %copy-done.4), channel_id=1, replica_groups=mesh['y'=4,'xl'=2,'c'=2,'z'=8,'xh'=2] {'z','c'}, dimensions={0}, use_global_device_ids=true | all-gather | bytes 835584 | tf_op jit(solution)/shard_map/all_gather | solution.py:337
  34.0 0.0 all-to-all-done.rows_ref
  34.0 5.9 %score.1 = (bf16[3072,3072]{1,0:T(8,128)(2,1)S(1)}, f32[32,128]{1,0:T(8,128)S(1)}) custom-call(s32[2]{0:T(128)S(1)} %pad_add_fusion.place_ref, bf16[16,192,128]{2,1,0:T(8,128)(2,1)S(1)} %all-to-all-done.rows_ref, bf16[3072,128]{1,0:T(8,128)(2,1)S(1)} %all_gather.9.columns_ref, f32[8,128]{1,0:T(8,128)S(1)} %copy-done.3), custom_call_target="tpu_custom_call" | custom-call | tf_op jit(solution)/shard_map/score/pallas_call | solution.py:137
  39.9 1.8 %all_gather.10.arrived_ref = f32[64,128]{1,0:T(8,128)S(1)} all-gather(f32[32,128]{1,0:T(8,128)S(1)} %get-tuple-element.21), channel_id=1, replica_groups=mesh['y'=4,'xl'=2,'c'=2,'z'=8,'xh'=2] {'c'}, dimensions={0}, use_global_device_ids=true | all-gather | bytes 49152 | tf_op jit(solution)/shard_map/all_gather | solution.py:340
  41.8 11.5 %all_to_all.30.partial_ref = f32[8,32,128]{2,1,0:T(8,128)S(1)} all-to-all(f32[8,32,128]{2,1,0:T(8,128)S(1)} %spread.1), channel_id=1, replica_groups=mesh['y'=4,'xl'=2,'c'=2,'z'=8,'xh'=2] {'z'}, dimensions={0} | all-to-all | bytes 262144 | tf_op jit(solution)/shard_map/all_to_all | solution.py:341
  53.3 5.8 %weigh.1 = (bf16[16,192,256]{2,1,0:T(8,128)(2,1)S(1)}, f32[192,128]{1,0:T(8,128)S(1)}, f32[8,128]{1,0:T(8,128)S(1)}) custom-call(s32[2]{0:T(128)S(1)} %pad_add_fusion.place_ref, f32[8,32,128]{2,1,0:T(8,128)S(1)} %all_to_all.30.partial_ref, bf16[3072,128]{1,0:T(8,128)(2,1)S(1)} %all_gather.9.columns_ref, bf16[3072,3072]{1,0:T(8,128)(2,1)S(1)} %get-tuple-element.22.powers_ref), custom_call_target="tpu_custom_call" | custom-call | tf_op jit(solution)/shard_map/weigh/pallas_call | solution.py:194
  59.1 0.0 copy-start
  59.1 0.0 copy-start.1
  59.1 26.3 %all_to_all.31.arrived_ref = bf16[16,192,256]{2,1,0:T(8,128)(2,1)S(1)} all-to-all(bf16[16,192,256]{2,1,0:T(8,128)(2,1)S(1)} %get-tuple-element.23), channel_id=1, replica_groups=mesh['y'=4,'xl'=2,'c'=2,'z'=8,'xh'=2] {'y','xl','xh'}, dimensions={0} | all-to-all | bytes 3145728 | tf_op jit(solution)/shard_map/all_to_all | solution.py:343
  85.5 0.9 gradient.1
  86.4 3.8 %collective-permute-start = (bf16[1024,128]{1,0:T(8,128)(2,1)S(1)}, bf16[1024,128]{1,0:T(8,128)(2,1)S(1)}, u32[]{:S(2)}, u32[]{:S(2)}) collective-permute-start(bf16[1024,128]{1,0:T(8,128)(2,1)S(1)} %get-tuple-element.28), channel_id=1, source_target_pairs={{0,16},{16,0},{1,17},{17,1},{2,18},{18,2},{3,19},{19,3},{4,20},{20... | collective-permute-start | bytes 786440 | tf_op jit(solution)/shard_map/ppermute | solution.py:345
  90.2 1.2 collective-permute-done.other_ref
  91.4 0.1 join.1
  91.4 10.5 %all_to_all.32.arrived_ref = bf16[16,64,128]{2,1,0:T(8,128)(2,1)S(1)} all-to-all(bf16[16,64,128]{2,1,0:T(8,128)(2,1)S(1)} %join.1), channel_id=1, replica_groups=mesh['y'=4,'xl'=2,'c'=2,'z'=8,'xh'=2] {'y','xl','xh'}, dimensions={0} | all-to-all | bytes 524288 | tf_op jit(solution)/shard_map/all_to_all | solution.py:346
  102.0 10.4 %all_to_all.33.arrived_ref = bf16[8,64,128]{2,1,0:T(8,128)(2,1)S(1)} all-to-all(bf16[8,64,128]{2,1,0:T(8,128)(2,1)S(1)} %share.1), channel_id=1, replica_groups=mesh['y'=4,'xl'=2,'c'=2,'z'=8,'xh'=2] {'z'}, dimensions={0} | all-to-all | bytes 262144 | tf_op jit(solution)/shard_map/all_to_all | solution.py:347
  112.4 10.8 %all_to_all.34 = bf16[16,80,128]{2,1,0:T(8,128)(2,1)S(1)} all-to-all(bf16[16,80,128]{2,1,0:T(8,128)(2,1)S(1)} %packet.1), channel_id=1, replica_groups=mesh['y'=4,'xl'=2,'c'=2,'z'=8,'xh'=2] {'y','xl','xh'}, dimensions={0} | all-to-all | bytes 655360 | tf_op jit(solution)/shard_map/all_to_all | solution.py:348
  123.2 6.1 %all_gather.11.arrived_ref = bf16[32,80,128]{2,1,0:T(8,128)(2,1)S(1)} all-gather(bf16[16,80,128]{2,1,0:T(8,128)(2,1)S(1)} %all_to_all.34), channel_id=1, replica_groups=mesh['y'=4,'xl'=2,'c'=2,'z'=8,'xh'=2] {'c'}, dimensions={0}, use_global_device_ids=true | all-gather | bytes 983040 | tf_op jit(solution)/shard_map/all_gather | solution.py:349
  129.4 1.0 finish.1
  (8 shorter events, 0.1 us)
Async XLA Ops:
  3.4 7.7 %copy-start.4 = (bf16[192,128]{1,0:T(8,128)(2,1)S(1)}, bf16[192,128]{1,0:T(8,128)(2,1)}, u32[]{:S(2)}) copy-start(bf16[192,128]{1,0:T(8,128)(2,1)} %get-tuple-element.19) | copy-start | bytes 147460
  3.4 30.6 %copy-start.3 = (f32[8,128]{1,0:T(8,128)S(1)}, f32[8,128]{1,0:T(8,128)}, u32[]{:S(2)}) copy-start(f32[8,128]{1,0:T(8,128)} %get-tuple-element.20.pair_sum_ref) | copy-start | bytes 12292
  3.4 30.6 %all-to-all-start = ((bf16[16,192,128]{2,1,0:T(8,128)(2,1)}), bf16[16,192,128]{2,1,0:T(8,128)(2,1)S(1)}, u32[]{:S(2)}, u32[]{:S(2)}) async-start(bf16[16,192,128]{2,1,0:T(8,128)(2,1)} %get-tuple-element.18), calls=%async_computation | async-start | bytes 1572864 | tf_op jit(solution)/shard_map/all_to_all | solution.py:338
  59.1 26.4 %copy-start = (bf16[192,2048]{1,0:T(8,128)(2,1)S(1)}, bf16[192,2048]{1,0:T(8,128)(2,1)}, u32[]{:S(2)}) copy-start(bf16[192,2048]{1,0:T(8,128)(2,1)} %hidden_ref.1) | copy-start | bytes 2359300
  59.1 26.4 %copy-start.1 = (f32[192,128]{1,0:T(8,128)S(1)}, f32[192,128]{1,0:T(8,128)}, u32[]{:S(2)}) copy-start(f32[192,128]{1,0:T(8,128)} %get-tuple-element.26.projected_ref) | copy-start | bytes 294916
  59.1 26.4 %copy-start.2 = (f32[192,128]{1,0:T(8,128)S(1)}, f32[192,128]{1,0:T(8,128)}, u32[]{:S(2)}) copy-start(f32[192,128]{1,0:T(8,128)} %get-tuple-element.25.pair_ref) | copy-start | bytes 294916
  86.4 5.0 %collective-permute-start = (bf16[1024,128]{1,0:T(8,128)(2,1)S(1)}, bf16[1024,128]{1,0:T(8,128)(2,1)S(1)}, u32[]{:S(2)}, u32[]{:S(2)}) collective-permute-start(bf16[1024,128]{1,0:T(8,128)(2,1)S(1)} %get-tuple-element.28), channel_id=1, source_target_pairs={{0,16},{16,0},{1,17},{17,1},{2,18},{18,2},{3,19},{19,3},{4,20},{20... | collective-permute-start | bytes 786440 | tf_op jit(solution)/shard_map/ppermute | solution.py:345

commit v5 on v4

--- a/solution.py
+++ b/solution.py
@@ -25,7 +25,7 @@
 
 VMEM = pl.BlockSpec(memory_space=pltpu.VMEM)
 SMEM = pl.BlockSpec(memory_space=pltpu.SMEM)
-ANY = pl.BlockSpec(memory_space=pl.ANY)
+HBM = pl.BlockSpec(memory_space=pltpu.HBM)
 
 
 def params(size):
@@ -81,7 +81,7 @@
 def project(hidden, weight, partner):
     return pl.pallas_call(
         project_body,
-        in_specs=[ANY] * 3,
+        in_specs=[HBM] * 3,
         out_specs=(VMEM,) * 5,
         out_shape=(
             jax.ShapeDtypeStruct((ROWS, WIDTH), jnp.float32),
@@ -168,7 +168,9 @@
     )(arrived)
 
 
-def weigh_body(place_ref, partial_ref, columns_ref, powers_ref, out_ref, own_ref, loss_ref, inverse, both):
+def weigh_body(
+    place_ref, partial_ref, columns_ref, powers_ref, out_hbm, own_ref, loss_ref, inverse, both, staged, sent
+):
     sums = jnp.sum(partial_ref[...], axis=0)
     totals = sums[:TILES, :]
     loss_ref[...] = total_of(jnp.log(totals)) - sums[TILES:, :]
@@ -182,27 +184,35 @@
         both[rows, WIDTH:] = (piece.astype(jnp.float32) * turned).astype(jnp.bfloat16)
     own_ref[...] = inverse[pl.ds(pl.multiple_of(place_ref[1] * ROWS, ROWS), ROWS), :]
     block = 4 * ROWS
+    copies = []
     for i in range(SPAN // block):
         weighed = jnp.dot(
             powers_ref[i * block : (i + 1) * block, :], both[...], preferred_element_type=jnp.float32
         ).astype(jnp.bfloat16)
-        for b in range(4):
-            out_ref[lax.rem(place_ref[0] + 4 * i + b, 16)] = weighed[b * ROWS : (b + 1) * ROWS, :]
+        for b in range(4 * i, 4 * i + 4):
+            staged[b] = weighed[(b - 4 * i) * ROWS : (b - 4 * i + 1) * ROWS, :]
+            shard = lax.rem(place_ref[0] + b, 16)
+            copies.append(pltpu.make_async_copy(staged.at[b], out_hbm.at[shard], sent.at[b]))
+            copies[-1].start()
+    for copy in copies:
+        copy.wait()
 
 
 def weigh(place, partial, columns, powers):
     return pl.pallas_call(
         weigh_body,
         in_specs=[SMEM] + [VMEM] * 3,
-        out_specs=(VMEM,) * 3,
-        out_shape=(
-            pltpu.VMEM((16, ROWS, 2 * WIDTH), jnp.bfloat16),
+        out_specs=(HBM, VMEM, VMEM),
+        out_shape=(
+            pltpu.HBM((16, ROWS, 2 * WIDTH), jnp.bfloat16),
             jax.ShapeDtypeStruct((ROWS, WIDTH), jnp.float32),
             jax.ShapeDtypeStruct((8, WIDTH), jnp.float32),
         ),
         scratch_shapes=[
             pltpu.VMEM((SPAN, WIDTH), jnp.float32),
             pltpu.VMEM((SPAN, 2 * WIDTH), jnp.bfloat16),
+            pltpu.VMEM((16, ROWS, 2 * WIDTH), jnp.bfloat16),
+            pltpu.SemaphoreType.DMA((16,)),
         ],
         compiler_params=params(20),
         name="weigh",

time: 131 us -> 132 us (level)
  no operation moved by 1% of the time
where the time goes in v5:
time: 132 us
  blocking collectives  101 us (77%)
  Pallas kernels  17.5 us (13%)
  starting transfers between devices  11.4 us (9%)
    all_to_all x1, blocking collectives, local(): arrived = lax.all_to_all(weighed, PLANE, 0, 0)  26.5 us
    all_gather x1, blocking collectives, local(): columns = lax.all_gather(features, COLUMN, axis=0, tiled=True)  22.9 us
    all_to_all x1, blocking collectives, local(): partial = lax.all_to_all(sums, 'z', 0, 0)  11.5 us
    all_to_all x1, blocking collectives, local(): packets = lax.all_to_all(packet(shares, loss), PLANE, 0, 0)  10.8 us
    all_to_all x1, blocking collectives, local(): shares = lax.all_to_all(join(own, other), PLANE, 0, 0)  10.5 us
    all_to_all x1, blocking collectives, local(): shares = lax.all_to_all(share(shares), 'z', 0, 0)  10.4 us
    all_to_all x1, starting transfers between devices, local(): rows = lax.all_to_all(copies, PLANE, 0, 0)  7.6 us
    pallas_call x1, Pallas kernels, weigh(): pl.pallas_call(weigh_body, in_specs=[SMEM] + [VMEM] * 3, out_specs=(HBM,...  6.75 us
  transfers between devices with their start and end apart: 2, of which 1 were waited for; matrix products, arithmetic and copies ran while one was open for 0% of the time, Pallas kernels for 0%

profile of v5, /device:TPU:1, one launch (start us, length us, event | category | flops | bytes accessed | tf_op | source)
XLA Modules:
  0.0 131.6 jit_solution(7683998526584028504)
XLA Ops:
  0.6 2.8 %project.1 = (f32[192,128]{1,0:T(8,128)}, bf16[192,128]{1,0:T(8,128)(2,1)}, bf16[16,192,128]{2,1,0:T(8,128)(2,1)}, f32[192,128]{1,0:T(8,128)}, f32[8,128]{1,0:T(8,128)}) custom-call(bf16[192,2048]{1,0:T(8,128)(2,1)} %hidden_ref.1, bf16[2048,128]{1,0:T(8,128)(2,1)} %weight_hbm.1, s32[1,192]{1,0:T(1,128)} %bitcast.6), custom_call_target="tpu_custom_call" | custom-call | tf_op jit(solution)/shard_map/project/pallas_call | solution.py:82
  3.4 0.0 copy-start.4
  3.4 0.0 copy-start.3
  3.4 7.6 %all-to-all-start = ((bf16[16,192,128]{2,1,0:T(8,128)(2,1)}), bf16[16,192,128]{2,1,0:T(8,128)(2,1)S(1)}, u32[]{:S(2)}, u32[]{:S(2)}) async-start(bf16[16,192,128]{2,1,0:T(8,128)(2,1)} %get-tuple-element.18), calls=%async_computation | async-start | bytes 1572864 | tf_op jit(solution)/shard_map/all_to_all | solution.py:348
  11.0 0.1 pad_add_fusion.place_ref
  11.1 22.9 %all_gather.9.columns_ref = bf16[3072,128]{1,0:T(8,128)(2,1)S(1)} all-gather(bf16[192,128]{1,0:T(8,128)(2,1)S(1)} %copy-done.4), channel_id=1, replica_groups=mesh['y'=4,'xl'=2,'c'=2,'z'=8,'xh'=2] {'z','c'}, dimensions={0}, use_global_device_ids=true | all-gather | bytes 835584 | tf_op jit(solution)/shard_map/all_gather | solution.py:347
  34.0 0.0 all-to-all-done.rows_ref
  34.0 0.0 copy-done.3
  34.0 5.9 %score.1 = (bf16[3072,3072]{1,0:T(8,128)(2,1)S(1)}, f32[32,128]{1,0:T(8,128)S(1)}) custom-call(s32[2]{0:T(128)S(1)} %pad_add_fusion.place_ref, bf16[16,192,128]{2,1,0:T(8,128)(2,1)S(1)} %all-to-all-done.rows_ref, bf16[3072,128]{1,0:T(8,128)(2,1)S(1)} %all_gather.9.columns_ref, f32[8,128]{1,0:T(8,128)S(1)} %copy-done.3), custom_call_target="tpu_custom_call" | custom-call | tf_op jit(solution)/shard_map/score/pallas_call | solution.py:137
  40.0 1.8 %all_gather.10.arrived_ref = f32[64,128]{1,0:T(8,128)S(1)} all-gather(f32[32,128]{1,0:T(8,128)S(1)} %get-tuple-element.21), channel_id=1, replica_groups=mesh['y'=4,'xl'=2,'c'=2,'z'=8,'xh'=2] {'c'}, dimensions={0}, use_global_device_ids=true | all-gather | bytes 49152 | tf_op jit(solution)/shard_map/all_gather | solution.py:350
  41.8 11.5 %all_to_all.30.partial_ref = f32[8,32,128]{2,1,0:T(8,128)S(1)} all-to-all(f32[8,32,128]{2,1,0:T(8,128)S(1)} %spread.1), channel_id=1, replica_groups=mesh['y'=4,'xl'=2,'c'=2,'z'=8,'xh'=2] {'z'}, dimensions={0} | all-to-all | bytes 262144 | tf_op jit(solution)/shard_map/all_to_all | solution.py:351
  53.3 6.7 %weigh.1 = (bf16[16,192,256]{2,1,0:T(8,128)(2,1)}, f32[192,128]{1,0:T(8,128)S(1)}, f32[8,128]{1,0:T(8,128)S(1)}) custom-call(s32[2]{0:T(128)S(1)} %pad_add_fusion.place_ref, f32[8,32,128]{2,1,0:T(8,128)S(1)} %all_to_all.30.partial_ref, bf16[3072,128]{1,0:T(8,128)(2,1)S(1)} %all_gather.9.columns_ref, bf16[3072,3072]{1,0:T(8,128)(2,1)S(1)} %get-tuple-element.22.powers_ref), custom_call_target="tpu_custom_call" | custom-call | tf_op jit(solution)/shard_map/weigh/pallas_call | solution.py:202
  60.1 0.0 copy-start
  60.1 0.0 copy-start.1
  60.1 26.5 %all_to_all.31.arrived_ref = bf16[16,192,256]{2,1,0:T(8,128)(2,1)S(1)} all-to-all(bf16[16,192,256]{2,1,0:T(8,128)(2,1)} %get-tuple-element.23), channel_id=1, replica_groups=mesh['y'=4,'xl'=2,'c'=2,'z'=8,'xh'=2] {'y','xl','xh'}, dimensions={0} | all-to-all | bytes 3145728 | tf_op jit(solution)/shard_map/all_to_all | solution.py:353
  86.6 0.9 gradient.1
  87.5 3.8 %collective-permute-start = (bf16[1024,128]{1,0:T(8,128)(2,1)S(1)}, bf16[1024,128]{1,0:T(8,128)(2,1)S(1)}, u32[]{:S(2)}, u32[]{:S(2)}) collective-permute-start(bf16[1024,128]{1,0:T(8,128)(2,1)S(1)} %get-tuple-element.28), channel_id=1, source_target_pairs={{0,16},{16,0},{1,17},{17,1},{2,18},{18,2},{3,19},{19,3},{4,20},{20... | collective-permute-start | bytes 786440 | tf_op jit(solution)/shard_map/ppermute | solution.py:355
  91.3 1.2 collective-permute-done.other_ref
  92.5 0.1 join.1
  92.6 10.5 %all_to_all.32.arrived_ref = bf16[16,64,128]{2,1,0:T(8,128)(2,1)S(1)} all-to-all(bf16[16,64,128]{2,1,0:T(8,128)(2,1)S(1)} %join.1), channel_id=1, replica_groups=mesh['y'=4,'xl'=2,'c'=2,'z'=8,'xh'=2] {'y','xl','xh'}, dimensions={0} | all-to-all | bytes 524288 | tf_op jit(solution)/shard_map/all_to_all | solution.py:356
  103.1 10.4 %all_to_all.33.arrived_ref = bf16[8,64,128]{2,1,0:T(8,128)(2,1)S(1)} all-to-all(bf16[8,64,128]{2,1,0:T(8,128)(2,1)S(1)} %share.1), channel_id=1, replica_groups=mesh['y'=4,'xl'=2,'c'=2,'z'=8,'xh'=2] {'z'}, dimensions={0} | all-to-all | bytes 262144 | tf_op jit(solution)/shard_map/all_to_all | solution.py:357
  113.5 10.8 %all_to_all.34 = bf16[16,80,128]{2,1,0:T(8,128)(2,1)S(1)} all-to-all(bf16[16,80,128]{2,1,0:T(8,128)(2,1)S(1)} %packet.1), channel_id=1, replica_groups=mesh['y'=4,'xl'=2,'c'=2,'z'=8,'xh'=2] {'y','xl','xh'}, dimensions={0} | all-to-all | bytes 655360 | tf_op jit(solution)/shard_map/all_to_all | solution.py:358
  124.4 6.1 %all_gather.11.arrived_ref = bf16[32,80,128]{2,1,0:T(8,128)(2,1)S(1)} all-gather(bf16[16,80,128]{2,1,0:T(8,128)(2,1)S(1)} %all_to_all.34), channel_id=1, replica_groups=mesh['y'=4,'xl'=2,'c'=2,'z'=8,'xh'=2] {'c'}, dimensions={0}, use_global_device_ids=true | all-gather | bytes 983040 | tf_op jit(solution)/shard_map/all_gather | solution.py:359
  130.5 1.0 finish.1
  (8 shorter events, 0.1 us)
Async XLA Ops:
  3.4 7.7 %copy-start.4 = (bf16[192,128]{1,0:T(8,128)(2,1)S(1)}, bf16[192,128]{1,0:T(8,128)(2,1)}, u32[]{:S(2)}) copy-start(bf16[192,128]{1,0:T(8,128)(2,1)} %get-tuple-element.19) | copy-start | bytes 147460
  3.4 30.6 %copy-start.3 = (f32[8,128]{1,0:T(8,128)S(1)}, f32[8,128]{1,0:T(8,128)}, u32[]{:S(2)}) copy-start(f32[8,128]{1,0:T(8,128)} %get-tuple-element.20.pair_sum_ref) | copy-start | bytes 12292
  3.4 30.6 %all-to-all-start = ((bf16[16,192,128]{2,1,0:T(8,128)(2,1)}), bf16[16,192,128]{2,1,0:T(8,128)(2,1)S(1)}, u32[]{:S(2)}, u32[]{:S(2)}) async-start(bf16[16,192,128]{2,1,0:T(8,128)(2,1)} %get-tuple-element.18), calls=%async_computation | async-start | bytes 1572864 | tf_op jit(solution)/shard_map/all_to_all | solution.py:348
  60.1 26.6 %copy-start = (bf16[192,2048]{1,0:T(8,128)(2,1)S(1)}, bf16[192,2048]{1,0:T(8,128)(2,1)}, u32[]{:S(2)}) copy-start(bf16[192,2048]{1,0:T(8,128)(2,1)} %hidden_ref.1) | copy-start | bytes 2359300
  60.1 26.5 %copy-start.1 = (f32[192,128]{1,0:T(8,128)S(1)}, f32[192,128]{1,0:T(8,128)}, u32[]{:S(2)}) copy-start(f32[192,128]{1,0:T(8,128)} %get-tuple-element.26.projected_ref) | copy-start | bytes 294916
  60.1 26.5 %copy-start.2 = (f32[192,128]{1,0:T(8,128)S(1)}, f32[192,128]{1,0:T(8,128)}, u32[]{:S(2)}) copy-start(f32[192,128]{1,0:T(8,128)} %get-tuple-element.25.pair_ref) | copy-start | bytes 294916
  87.5 5.0 %collective-permute-start = (bf16[1024,128]{1,0:T(8,128)(2,1)S(1)}, bf16[1024,128]{1,0:T(8,128)(2,1)S(1)}, u32[]{:S(2)}, u32[]{:S(2)}) collective-permute-start(bf16[1024,128]{1,0:T(8,128)(2,1)S(1)} %get-tuple-element.28), channel_id=1, source_target_pairs={{0,16},{16,0},{1,17},{17,1},{2,18},{18,2},{3,19},{19,3},{4,20},{20... | collective-permute-start | bytes 786440 | tf_op jit(solution)/shard_map/ppermute | solution.py:355

commit v6 on v4

--- a/solution.py
+++ b/solution.py
@@ -10,9 +10,10 @@
 norm_epsilon = 1e-06
 log2_e = 1.4426950408889634
 
-AXES = ("y", "xl", "c", "z", "xh")
+AXES = ("y", "xl", "c", "zh", "zm", "zl", "xh")
 PLANE = ("y", "xl", "xh")
-COLUMN = ("z", "c")
+COLUMN = ("zh", "zm", "zl", "c")
+DEPTH = ("zl", "zm", "zh")
 ROWS = 192
 WIDTH = 128
 D_IN = 2048
@@ -20,12 +21,12 @@
 TILES = SPAN // WIDTH
 SHARE = D_IN // 32
 HALF = D_IN // 2
-PIECES = 2
+PIECES = 4
 MEBI = 1024 * 1024
 
 VMEM = pl.BlockSpec(memory_space=pltpu.VMEM)
 SMEM = pl.BlockSpec(memory_space=pltpu.SMEM)
-ANY = pl.BlockSpec(memory_space=pl.ANY)
+HBM = pl.BlockSpec(memory_space=pltpu.HBM)
 
 
 def params(size):
@@ -37,8 +38,8 @@
 
 
 def project_body(
-    hidden_hbm, weight_hbm, partner_hbm, projected_ref, features_ref, copies_ref, pair_ref, pair_sum_ref,
-    hidden, weight, partner, hidden_done, weight_done, partner_done,
+    hidden_hbm, weight_hbm, partner_hbm, projected_ref, features_ref, copies_hbm, pair_ref, pair_sum_ref,
+    hidden, weight, partner, staged, hidden_done, weight_done, partner_done, sent,
 ):
     depth = D_IN // PIECES
     copies = []
@@ -63,9 +64,11 @@
         projected += jnp.dot(hidden[:, part], weight[part, :], preferred_element_type=jnp.float32)
     inverse_norm = lax.rsqrt(jnp.sum(projected * projected, axis=1, keepdims=True) + norm_epsilon)
     features = (projected * inverse_norm).astype(jnp.bfloat16)
+    staged[...] = features
+    sends = [pltpu.make_async_copy(staged, copies_hbm.at[k], sent.at[k]) for k in range(16)]
+    for send in sends:
+        send.start()
     features_ref[...] = features
-    for k in range(16):
-        copies_ref[k] = features
     partner_copy.wait()
     places = lax.rem(partner[...], ROWS)
     picks = lax.broadcasted_iota(jnp.int32, (ROWS, ROWS), 0) == places
@@ -76,17 +79,19 @@
     pair_ref[...] = paired
     total = total_of(features.astype(jnp.float32) * paired)
     pair_sum_ref[...] = jnp.broadcast_to(inverse_tau * total, (8, WIDTH))
+    for send in sends:
+        send.wait()
 
 
 def project(hidden, weight, partner):
     return pl.pallas_call(
         project_body,
-        in_specs=[ANY] * 3,
-        out_specs=(VMEM,) * 5,
+        in_specs=[HBM] * 3,
+        out_specs=(VMEM, VMEM, HBM, VMEM, VMEM),
         out_shape=(
             jax.ShapeDtypeStruct((ROWS, WIDTH), jnp.float32),
             jax.ShapeDtypeStruct((ROWS, WIDTH), jnp.bfloat16),
-            pltpu.VMEM((16, ROWS, WIDTH), jnp.bfloat16),
+            pltpu.HBM((16, ROWS, WIDTH), jnp.bfloat16),
             jax.ShapeDtypeStruct((ROWS, WIDTH), jnp.float32),
             jax.ShapeDtypeStruct((8, WIDTH), jnp.float32),
         ),
@@ -94,9 +99,11 @@
             pltpu.VMEM((ROWS, D_IN), jnp.bfloat16),
             pltpu.VMEM((D_IN, WIDTH), jnp.bfloat16),
             pltpu.VMEM((1, ROWS), jnp.int32),
+            pltpu.VMEM((ROWS, WIDTH), jnp.bfloat16),
             pltpu.SemaphoreType.DMA((PIECES,)),
             pltpu.SemaphoreType.DMA((PIECES,)),
             pltpu.SemaphoreType.DMA,
+            pltpu.SemaphoreType.DMA((16,)),
         ],
         compiler_params=params(60),
         name="project",
@@ -238,7 +245,7 @@
         in_specs=[SMEM] + [VMEM] * 5,
         out_specs=(VMEM,) * 3,
         out_shape=(
-            jax.ShapeDtypeStruct((ROWS, WIDTH), jnp.float32),
+            pltpu.VMEM((ROWS, WIDTH), jnp.float32),
             pltpu.VMEM((HALF, WIDTH), jnp.float32),
             pltpu.VMEM((HALF, WIDTH), jnp.bfloat16),
         ),
@@ -329,7 +336,8 @@
 
 def local(hidden, weight, partner):
     plane_place = (lax.axis_index("y") * 2 + lax.axis_index("xl")) * 2 + lax.axis_index("xh")
-    column_place = lax.axis_index("z") * 2 + lax.axis_index("c")
+    deep_place = (lax.axis_index("zh") * 2 + lax.axis_index("zm")) * 2 + lax.axis_index("zl")
+    column_place = deep_place * 2 + lax.axis_index("c")
     core = lax.axis_index("c").astype(jnp.int32).reshape(1)
     place = jnp.stack([plane_place, column_place]).astype(jnp.int32)
 
@@ -338,13 +346,13 @@
     rows = lax.all_to_all(copies, PLANE, 0, 0)
     powers, sums = score(place, rows, columns, pair_sum)
     sums = spread(lax.all_gather(sums, "c", axis=0, tiled=True))
-    partial = lax.all_to_all(sums, "z", 0, 0)
+    partial = lax.all_to_all(sums, DEPTH, 0, 0)
     weighed, inverse, loss = weigh(place, partial, columns, powers)
     arrived = lax.all_to_all(weighed, PLANE, 0, 0)
     derivative, own, other = gradient(core, arrived, inverse, pair, projected, hidden)
     other = lax.ppermute(other, "c", [(0, 1), (1, 0)])
     shares = lax.all_to_all(join(own, other), PLANE, 0, 0)
-    shares = lax.all_to_all(share(shares), "z", 0, 0)
+    shares = lax.all_to_all(share(shares), DEPTH, 0, 0)
     packets = lax.all_to_all(packet(shares, loss), PLANE, 0, 0)
     packets = lax.all_gather(packets, "c", axis=0, tiled=True)
     mean_loss, grad_weight = finish(packets)
@@ -352,7 +360,7 @@
 
 
 def solution(mesh):
-    split = Mesh(mesh.devices.reshape(4, 2, 2, 8, 2), AXES)
+    split = Mesh(mesh.devices.reshape(4, 2, 2, 2, 2, 2, 2), AXES)
     return jax.shard_map(
         local,
         mesh=split,

time: 131 us -> 132 us (level)
  blocking collectives: 100 us -> 88.4 us
  waiting for transfers between devices: 1.16 us -> 8.05 us
  starting transfers between devices: 11.4 us -> 15.3 us
  Pallas kernels: 16.6 us -> 18.1 us
    all_to_all x3 -> x2, blocking collectives: 32.7 us -> 20.2 us  [the longest x1 10.3 us: local(): shares = lax.all_to_all(share(shares), DEPTH, 0, 0)]
    all_to_all x0 -> x1, waiting for transfers between devices: none -> 6.88 us  [local(): packets = lax.all_to_all(packet(shares, loss), PLANE, 0, 0)]
    all_to_all x0 -> x1, starting transfers between devices: none -> 3.66 us  [local(): packets = lax.all_to_all(packet(shares, loss), PLANE, 0, 0)]
  transfers between devices with their start and end apart: 2 -> 3, of which waited for: 1 -> 2; matrix products, arithmetic and copies ran while one was open for 0% -> 1% of each run, Pallas kernels for 0% -> 0%
where the time goes in v6:
time: 132 us; the launch traced here: 131 us
  blocking collectives  88.4 us (67%)
  Pallas kernels  18.1 us (14%)
  starting transfers between devices  15.3 us (12%)
  waiting for transfers between devices  8.05 us (6%)
    all_to_all x1, blocking collectives, local(): arrived = lax.all_to_all(weighed, PLANE, 0, 0)  26.3 us
    all_gather x1, blocking collectives, local(): columns = lax.all_gather(features, COLUMN, axis=0, tiled=True)  22.9 us
    all_to_all x1, blocking collectives, local(): shares = lax.all_to_all(join(own, other), PLANE, 0, 0)  10.8 us
    all_to_all x1, blocking collectives, local(): shares = lax.all_to_all(share(shares), DEPTH, 0, 0)  10.3 us
    all_to_all x1, blocking collectives, local(): partial = lax.all_to_all(sums, DEPTH, 0, 0)  9.89 us
    all_to_all x1, starting transfers between devices, local(): rows = lax.all_to_all(copies, PLANE, 0, 0)  7.6 us
    all_to_all x1, waiting for transfers between devices, local(): packets = lax.all_to_all(packet(shares, loss), PLANE, 0, 0)  6.88 us
    all_gather x1, blocking collectives, local(): packets = lax.all_gather(packets, 'c', axis=0, tiled=True)  6.36 us
  transfers between devices with their start and end apart: 3, of which 2 were waited for; matrix products, arithmetic and copies ran while one was open for 1% of the time, Pallas kernels for 0%

profile of v6, /device:TPU:1, one launch (start us, length us, event | category | flops | bytes accessed | tf_op | source)
XLA Modules:
  0.0 131.3 jit_solution(5969196442451431368)
XLA Ops:
  0.6 3.7 %project.1 = (f32[192,128]{1,0:T(8,128)}, bf16[192,128]{1,0:T(8,128)(2,1)}, bf16[16,192,128]{2,1,0:T(8,128)(2,1)}, f32[192,128]{1,0:T(8,128)}, f32[8,128]{1,0:T(8,128)}) custom-call(bf16[192,2048]{1,0:T(8,128)(2,1)} %hidden_ref.1, bf16[2048,128]{1,0:T(8,128)(2,1)} %weight_hbm.1, s32[1,192]{1,0:T(1,128)} %bitcast.6), custom_call_target="tpu_custom_call" | custom-call | tf_op jit(solution)/shard_map/project/pallas_call | solution.py:87
  4.4 7.6 %all-to-all-start = ((bf16[16,192,128]{2,1,0:T(8,128)(2,1)}), bf16[16,192,128]{2,1,0:T(8,128)(2,1)S(1)}, u32[]{:S(2)}, u32[]{:S(2)}) async-start(bf16[16,192,128]{2,1,0:T(8,128)(2,1)} %get-tuple-element.18), calls=%async_computation | async-start | bytes 1572864 | tf_op jit(solution)/shard_map/all_to_all | solution.py:346
  12.0 0.1 pad_add_fusion.place_ref
  12.1 22.9 %all_gather.9.columns_ref = bf16[3072,128]{1,0:T(8,128)(2,1)S(1)} all-gather(bf16[192,128]{1,0:T(8,128)(2,1)S(1)} %copy-done.4), channel_id=1, replica_groups=mesh['y'=4,'xl'=2,'c'=2,'zh'=2,'zm'=2,'zl'=2,'xh'=2] {'zh','zm','zl','c'}, dimensions={0}, use_global_device_ids=true | all-gather | bytes 835584 | tf_op jit(solution)/shard_map/all_gather | solution.py:345
  34.9 0.0 all-to-all-done.rows_ref
  35.0 5.9 %score.1 = (bf16[3072,3072]{1,0:T(8,128)(2,1)S(1)}, f32[32,128]{1,0:T(8,128)S(1)}) custom-call(s32[2]{0:T(128)S(1)} %pad_add_fusion.place_ref, bf16[16,192,128]{2,1,0:T(8,128)(2,1)S(1)} %all-to-all-done.rows_ref, bf16[3072,128]{1,0:T(8,128)(2,1)S(1)} %all_gather.9.columns_ref, f32[8,128]{1,0:T(8,128)S(1)} %copy-done.3), custom_call_target="tpu_custom_call" | custom-call | tf_op jit(solution)/shard_map/score/pallas_call | solution.py:144
  40.9 1.8 %all_gather.10.arrived_ref = f32[64,128]{1,0:T(8,128)S(1)} all-gather(f32[32,128]{1,0:T(8,128)S(1)} %get-tuple-element.21), channel_id=1, replica_groups=mesh['y'=4,'xl'=2,'c'=2,'zh'=2,'zm'=2,'zl'=2,'xh'=2] {'c'}, dimensions={0}, use_global_device_ids=true | all-gather | bytes 49152 | tf_op jit(solution)/shard_map/all_gather | solution.py:348
  42.7 9.9 %all_to_all.30.partial_ref = f32[8,32,128]{2,1,0:T(8,128)S(1)} all-to-all(f32[8,32,128]{2,1,0:T(8,128)S(1)} %spread.1), channel_id=1, replica_groups=mesh['y'=4,'xl'=2,'c'=2,'zh'=2,'zm'=2,'zl'=2,'xh'=2] {'zl','zm','zh'}, dimensions={0} | all-to-all | bytes 262144 | tf_op jit(solution)/shard_map/all_to_all | solution.py:349
  52.6 5.8 %weigh.1 = (bf16[16,192,256]{2,1,0:T(8,128)(2,1)S(1)}, f32[192,128]{1,0:T(8,128)S(1)}, f32[8,128]{1,0:T(8,128)S(1)}) custom-call(s32[2]{0:T(128)S(1)} %pad_add_fusion.place_ref, f32[8,32,128]{2,1,0:T(8,128)S(1)} %all_to_all.30.partial_ref, bf16[3072,128]{1,0:T(8,128)(2,1)S(1)} %all_gather.9.columns_ref, bf16[3072,3072]{1,0:T(8,128)(2,1)S(1)} %get-tuple-element.22.powers_ref), custom_call_target="tpu_custom_call" | custom-call | tf_op jit(solution)/shard_map/weigh/pallas_call | solution.py:201
  58.4 0.0 copy-start
  58.5 0.0 copy-start.1
  58.5 26.3 %all_to_all.31.arrived_ref = bf16[16,192,256]{2,1,0:T(8,128)(2,1)S(1)} all-to-all(bf16[16,192,256]{2,1,0:T(8,128)(2,1)S(1)} %get-tuple-element.23), channel_id=1, replica_groups=mesh['y'=4,'xl'=2,'c'=2,'zh'=2,'zm'=2,'zl'=2,'xh'=2] {'y','xl','xh'}, dimensions={0} | all-to-all | bytes 3145728 | tf_op jit(solution)/shard_map/all_to_all | solution.py:351
  84.8 0.0 copy-done.2
  84.8 0.7 gradient.1
  85.6 4.0 %collective-permute-start = (bf16[1024,128]{1,0:T(8,128)(2,1)S(1)}, bf16[1024,128]{1,0:T(8,128)(2,1)S(1)}, u32[]{:S(2)}, u32[]{:S(2)}) collective-permute-start(bf16[1024,128]{1,0:T(8,128)(2,1)S(1)} %get-tuple-element.28), channel_id=1, source_target_pairs={{0,16},{16,0},{1,17},{17,1},{2,18},{18,2},{3,19},{19,3},{4,20},{20... | collective-permute-start | bytes 786440 | tf_op jit(solution)/shard_map/ppermute | solution.py:353
  89.6 1.2 collective-permute-done.other_ref
  90.8 10.8 %all_to_all.32.arrived_ref = bf16[16,64,128]{2,1,0:T(8,128)(2,1)S(1)} all-to-all(bf16[16,64,128]{2,1,0:T(8,128)(2,1)S(1)} %join.1), channel_id=1, replica_groups=mesh['y'=4,'xl'=2,'c'=2,'zh'=2,'zm'=2,'zl'=2,'xh'=2] {'y','xl','xh'}, dimensions={0} | all-to-all | bytes 524288 | tf_op jit(solution)/shard_map/all_to_all | solution.py:354
  101.6 10.3 %all_to_all.33.arrived_ref = bf16[8,64,128]{2,1,0:T(8,128)(2,1)S(1)} all-to-all(bf16[8,64,128]{2,1,0:T(8,128)(2,1)S(1)} %share.1), channel_id=1, replica_groups=mesh['y'=4,'xl'=2,'c'=2,'zh'=2,'zm'=2,'zl'=2,'xh'=2] {'zl','zm','zh'}, dimensions={0} | all-to-all | bytes 262144 | tf_op jit(solution)/shard_map/all_to_all | solution.py:355
  112.0 0.8 packet.1
  112.7 3.7 %all-to-all-start.5 = ((bf16[16,80,128]{2,1,0:T(8,128)(2,1)}), bf16[16,80,128]{2,1,0:T(8,128)(2,1)S(1)}, u32[]{:S(2)}, u32[]{:S(2)}) async-start(bf16[16,80,128]{2,1,0:T(8,128)(2,1)} %packet.1), calls=%async_computation.5 | async-start | bytes 655360 | tf_op jit(solution)/shard_map/all_to_all | solution.py:356
  116.4 0.6 copy.6
  117.0 6.9 %all-to-all-done.5 = bf16[16,80,128]{2,1,0:T(8,128)(2,1)S(1)} async-done(((bf16[16,80,128]{2,1,0:T(8,128)(2,1)}), bf16[16,80,128]{2,1,0:T(8,128)(2,1)S(1)}, u32[]{:S(2)}, u32[]{:S(2)}) %all-to-all-start.5) | async-done | bytes 327712 | tf_op jit(solution)/shard_map/all_to_all | solution.py:356
  123.9 6.4 %all_gather.11.arrived_ref = bf16[32,80,128]{2,1,0:T(8,128)(2,1)S(1)} all-gather(bf16[16,80,128]{2,1,0:T(8,128)(2,1)S(1)} %all-to-all-done.5), channel_id=1, replica_groups=mesh['y'=4,'xl'=2,'c'=2,'zh'=2,'zm'=2,'zl'=2,'xh'=2] {'c'}, dimensions={0}, use_global_device_ids=true | all-gather | bytes 983040 | tf_op jit(solution)/shard_map/all_gather | solution.py:357
  130.3 1.0 finish.1
  (10 shorter events, 0.1 us)
Async XLA Ops:
  4.3 7.7 %copy-start.4 = (bf16[192,128]{1,0:T(8,128)(2,1)S(1)}, bf16[192,128]{1,0:T(8,128)(2,1)}, u32[]{:S(2)}) copy-start(bf16[192,128]{1,0:T(8,128)(2,1)} %get-tuple-element.19) | copy-start | bytes 147460
  4.3 30.6 %copy-start.3 = (f32[8,128]{1,0:T(8,128)S(1)}, f32[8,128]{1,0:T(8,128)}, u32[]{:S(2)}) copy-start(f32[8,128]{1,0:T(8,128)} %get-tuple-element.20.pair_sum_ref) | copy-start | bytes 12292
  4.4 30.6 %all-to-all-start = ((bf16[16,192,128]{2,1,0:T(8,128)(2,1)}), bf16[16,192,128]{2,1,0:T(8,128)(2,1)S(1)}, u32[]{:S(2)}, u32[]{:S(2)}) async-start(bf16[16,192,128]{2,1,0:T(8,128)(2,1)} %get-tuple-element.18), calls=%async_computation | async-start | bytes 1572864 | tf_op jit(solution)/shard_map/all_to_all | solution.py:346
  58.4 26.4 %copy-start = (bf16[192,2048]{1,0:T(8,128)(2,1)S(1)}, bf16[192,2048]{1,0:T(8,128)(2,1)}, u32[]{:S(2)}) copy-start(bf16[192,2048]{1,0:T(8,128)(2,1)} %hidden_ref.1) | copy-start | bytes 2359300
  58.5 26.4 %copy-start.1 = (f32[192,128]{1,0:T(8,128)S(1)}, f32[192,128]{1,0:T(8,128)}, u32[]{:S(2)}) copy-start(f32[192,128]{1,0:T(8,128)} %get-tuple-element.26.projected_ref) | copy-start | bytes 294916
  58.5 26.4 %copy-start.2 = (f32[192,128]{1,0:T(8,128)S(1)}, f32[192,128]{1,0:T(8,128)}, u32[]{:S(2)}) copy-start(f32[192,128]{1,0:T(8,128)} %get-tuple-element.25.pair_ref) | copy-start | bytes 294916
  85.6 5.2 %collective-permute-start = (bf16[1024,128]{1,0:T(8,128)(2,1)S(1)}, bf16[1024,128]{1,0:T(8,128)(2,1)S(1)}, u32[]{:S(2)}, u32[]{:S(2)}) collective-permute-start(bf16[1024,128]{1,0:T(8,128)(2,1)S(1)} %get-tuple-element.28), channel_id=1, source_target_pairs={{0,16},{16,0},{1,17},{17,1},{2,18},{18,2},{3,19},{19,3},{4,20},{20... | collective-permute-start | bytes 786440 | tf_op jit(solution)/shard_map/ppermute | solution.py:353
  112.7 11.2 %all-to-all-start.5 = ((bf16[16,80,128]{2,1,0:T(8,128)(2,1)}), bf16[16,80,128]{2,1,0:T(8,128)(2,1)S(1)}, u32[]{:S(2)}, u32[]{:S(2)}) async-start(bf16[16,80,128]{2,1,0:T(8,128)(2,1)} %packet.1), calls=%async_computation.5 | async-start | bytes 655360 | tf_op jit(solution)/shard_map/all_to_all | solution.py:356

commit v7 on v4

--- a/solution.py
+++ b/solution.py
@@ -11,7 +11,7 @@
 log2_e = 1.4426950408889634
 
 AXES = ("y", "xl", "c", "z", "xh")
-PLANE = ("y", "xl", "xh")
+PLANE = ("xl", "xh", "y")
 COLUMN = ("z", "c")
 ROWS = 192
 WIDTH = 128
@@ -328,7 +328,7 @@
 
 
 def local(hidden, weight, partner):
-    plane_place = (lax.axis_index("y") * 2 + lax.axis_index("xl")) * 2 + lax.axis_index("xh")
+    plane_place = (lax.axis_index("xl") * 2 + lax.axis_index("xh")) * 4 + lax.axis_index("y")
     column_place = lax.axis_index("z") * 2 + lax.axis_index("c")
     core = lax.axis_index("c").astype(jnp.int32).reshape(1)
     place = jnp.stack([plane_place, column_place]).astype(jnp.int32)

time: 131 us -> 131 us (level)
  no operation moved by 1% of the time
where the time goes in v7:
time: 131 us; the launch traced here: 130 us
  blocking collectives  101 us (77%)
  Pallas kernels  16.6 us (13%)
  starting transfers between devices  11 us (8%)
    all_to_all x1, blocking collectives, local(): arrived = lax.all_to_all(weighed, PLANE, 0, 0)  26.8 us
    all_gather x1, blocking collectives, local(): columns = lax.all_gather(features, COLUMN, axis=0, tiled=True)  22.9 us
    all_to_all x1, blocking collectives, local(): partial = lax.all_to_all(sums, 'z', 0, 0)  11.5 us
    all_to_all x1, blocking collectives, local(): shares = lax.all_to_all(join(own, other), PLANE, 0, 0)  10.6 us
    all_to_all x1, blocking collectives, local(): packets = lax.all_to_all(packet(shares, loss), PLANE, 0, 0)  10.5 us
    all_to_all x1, blocking collectives, local(): shares = lax.all_to_all(share(shares), 'z', 0, 0)  10.3 us
    all_to_all x1, starting transfers between devices, local(): rows = lax.all_to_all(copies, PLANE, 0, 0)  7.6 us
    all_gather x1, blocking collectives, local(): packets = lax.all_gather(packets, 'c', axis=0, tiled=True)  6.25 us
  transfers between devices with their start and end apart: 2, of which 1 were waited for; matrix products, arithmetic and copies ran while one was open for 0% of the time, Pallas kernels for 0%

profile of v7, /device:TPU:1, one launch (start us, length us, event | category | flops | bytes accessed | tf_op | source)
XLA Modules:
  0.0 130.3 jit_solution(365914708191700428)
XLA Ops:
  0.6 2.8 %project.1 = (f32[192,128]{1,0:T(8,128)}, bf16[192,128]{1,0:T(8,128)(2,1)}, bf16[16,192,128]{2,1,0:T(8,128)(2,1)}, f32[192,128]{1,0:T(8,128)}, f32[8,128]{1,0:T(8,128)}) custom-call(bf16[192,2048]{1,0:T(8,128)(2,1)} %hidden_ref.1, bf16[2048,128]{1,0:T(8,128)(2,1)} %weight_hbm.1, s32[1,192]{1,0:T(1,128)} %bitcast.6), custom_call_target="tpu_custom_call" | custom-call | tf_op jit(solution)/shard_map/project/pallas_call | solution.py:82
  3.4 0.0 copy-start.4
  3.4 0.0 copy-start.3
  3.4 7.6 %all-to-all-start = ((bf16[16,192,128]{2,1,0:T(8,128)(2,1)}), bf16[16,192,128]{2,1,0:T(8,128)(2,1)S(1)}, u32[]{:S(2)}, u32[]{:S(2)}) async-start(bf16[16,192,128]{2,1,0:T(8,128)(2,1)} %get-tuple-element.18), calls=%async_computation | async-start | bytes 1572864 | tf_op jit(solution)/shard_map/all_to_all | solution.py:338
  11.0 0.1 pad_add_fusion.place_ref
  11.1 22.9 %all_gather.9.columns_ref = bf16[3072,128]{1,0:T(8,128)(2,1)S(1)} all-gather(bf16[192,128]{1,0:T(8,128)(2,1)S(1)} %copy-done.4), channel_id=1, replica_groups=mesh['y'=4,'xl'=2,'c'=2,'z'=8,'xh'=2] {'z','c'}, dimensions={0}, use_global_device_ids=true | all-gather | bytes 835584 | tf_op jit(solution)/shard_map/all_gather | solution.py:337
  34.0 0.0 all-to-all-done.rows_ref
  34.0 5.9 %score.1 = (bf16[3072,3072]{1,0:T(8,128)(2,1)S(1)}, f32[32,128]{1,0:T(8,128)S(1)}) custom-call(s32[2]{0:T(128)S(1)} %pad_add_fusion.place_ref, bf16[16,192,128]{2,1,0:T(8,128)(2,1)S(1)} %all-to-all-done.rows_ref, bf16[3072,128]{1,0:T(8,128)(2,1)S(1)} %all_gather.9.columns_ref, f32[8,128]{1,0:T(8,128)S(1)} %copy-done.3), custom_call_target="tpu_custom_call" | custom-call | tf_op jit(solution)/shard_map/score/pallas_call | solution.py:137
  39.9 1.8 %all_gather.10.arrived_ref = f32[64,128]{1,0:T(8,128)S(1)} all-gather(f32[32,128]{1,0:T(8,128)S(1)} %get-tuple-element.21), channel_id=1, replica_groups=mesh['y'=4,'xl'=2,'c'=2,'z'=8,'xh'=2] {'c'}, dimensions={0}, use_global_device_ids=true | all-gather | bytes 49152 | tf_op jit(solution)/shard_map/all_gather | solution.py:340
  41.8 11.5 %all_to_all.30.partial_ref = f32[8,32,128]{2,1,0:T(8,128)S(1)} all-to-all(f32[8,32,128]{2,1,0:T(8,128)S(1)} %spread.1), channel_id=1, replica_groups=mesh['y'=4,'xl'=2,'c'=2,'z'=8,'xh'=2] {'z'}, dimensions={0} | all-to-all | bytes 262144 | tf_op jit(solution)/shard_map/all_to_all | solution.py:341
  53.3 5.8 %weigh.1 = (bf16[16,192,256]{2,1,0:T(8,128)(2,1)S(1)}, f32[192,128]{1,0:T(8,128)S(1)}, f32[8,128]{1,0:T(8,128)S(1)}) custom-call(s32[2]{0:T(128)S(1)} %pad_add_fusion.place_ref, f32[8,32,128]{2,1,0:T(8,128)S(1)} %all_to_all.30.partial_ref, bf16[3072,128]{1,0:T(8,128)(2,1)S(1)} %all_gather.9.columns_ref, bf16[3072,3072]{1,0:T(8,128)(2,1)S(1)} %get-tuple-element.22.powers_ref), custom_call_target="tpu_custom_call" | custom-call | tf_op jit(solution)/shard_map/weigh/pallas_call | solution.py:194
  59.1 0.0 copy-start
  59.1 0.0 copy-start.1
  59.1 26.8 %all_to_all.31.arrived_ref = bf16[16,192,256]{2,1,0:T(8,128)(2,1)S(1)} all-to-all(bf16[16,192,256]{2,1,0:T(8,128)(2,1)S(1)} %get-tuple-element.23), channel_id=1, replica_groups=mesh['y'=4,'xl'=2,'c'=2,'z'=8,'xh'=2] {'xl','xh','y'}, dimensions={0} | all-to-all | bytes 3145728 | tf_op jit(solution)/shard_map/all_to_all | solution.py:343
  86.0 0.0 copy-done.1
  86.0 0.9 gradient.1
  86.9 3.4 %collective-permute-start = (bf16[1024,128]{1,0:T(8,128)(2,1)S(1)}, bf16[1024,128]{1,0:T(8,128)(2,1)S(1)}, u32[]{:S(2)}, u32[]{:S(2)}) collective-permute-start(bf16[1024,128]{1,0:T(8,128)(2,1)S(1)} %get-tuple-element.28), channel_id=1, source_target_pairs={{0,16},{16,0},{1,17},{17,1},{2,18},{18,2},{3,19},{19,3},{4,20},{20... | collective-permute-start | bytes 786440 | tf_op jit(solution)/shard_map/ppermute | solution.py:345
  90.2 1.2 collective-permute-done.other_ref
  91.4 0.1 join.1
  91.5 10.6 %all_to_all.32.arrived_ref = bf16[16,64,128]{2,1,0:T(8,128)(2,1)S(1)} all-to-all(bf16[16,64,128]{2,1,0:T(8,128)(2,1)S(1)} %join.1), channel_id=1, replica_groups=mesh['y'=4,'xl'=2,'c'=2,'z'=8,'xh'=2] {'xl','xh','y'}, dimensions={0} | all-to-all | bytes 524288 | tf_op jit(solution)/shard_map/all_to_all | solution.py:346
  102.1 10.3 %all_to_all.33.arrived_ref = bf16[8,64,128]{2,1,0:T(8,128)(2,1)S(1)} all-to-all(bf16[8,64,128]{2,1,0:T(8,128)(2,1)S(1)} %share.1), channel_id=1, replica_groups=mesh['y'=4,'xl'=2,'c'=2,'z'=8,'xh'=2] {'z'}, dimensions={0} | all-to-all | bytes 262144 | tf_op jit(solution)/shard_map/all_to_all | solution.py:347
  112.5 10.5 %all_to_all.34 = bf16[16,80,128]{2,1,0:T(8,128)(2,1)S(1)} all-to-all(bf16[16,80,128]{2,1,0:T(8,128)(2,1)S(1)} %packet.1), channel_id=1, replica_groups=mesh['y'=4,'xl'=2,'c'=2,'z'=8,'xh'=2] {'xl','xh','y'}, dimensions={0} | all-to-all | bytes 655360 | tf_op jit(solution)/shard_map/all_to_all | solution.py:348
  123.0 6.2 %all_gather.11.arrived_ref = bf16[32,80,128]{2,1,0:T(8,128)(2,1)S(1)} all-gather(bf16[16,80,128]{2,1,0:T(8,128)(2,1)S(1)} %all_to_all.34), channel_id=1, replica_groups=mesh['y'=4,'xl'=2,'c'=2,'z'=8,'xh'=2] {'c'}, dimensions={0}, use_global_device_ids=true | all-gather | bytes 983040 | tf_op jit(solution)/shard_map/all_gather | solution.py:349
  129.2 1.0 finish.1
  (8 shorter events, 0.1 us)
Async XLA Ops:
  3.4 7.7 %copy-start.4 = (bf16[192,128]{1,0:T(8,128)(2,1)S(1)}, bf16[192,128]{1,0:T(8,128)(2,1)}, u32[]{:S(2)}) copy-start(bf16[192,128]{1,0:T(8,128)(2,1)} %get-tuple-element.19) | copy-start | bytes 147460
  3.4 30.6 %copy-start.3 = (f32[8,128]{1,0:T(8,128)S(1)}, f32[8,128]{1,0:T(8,128)}, u32[]{:S(2)}) copy-start(f32[8,128]{1,0:T(8,128)} %get-tuple-element.20.pair_sum_ref) | copy-start | bytes 12292
  3.4 30.6 %all-to-all-start = ((bf16[16,192,128]{2,1,0:T(8,128)(2,1)}), bf16[16,192,128]{2,1,0:T(8,128)(2,1)S(1)}, u32[]{:S(2)}, u32[]{:S(2)}) async-start(bf16[16,192,128]{2,1,0:T(8,128)(2,1)} %get-tuple-element.18), calls=%async_computation | async-start | bytes 1572864 | tf_op jit(solution)/shard_map/all_to_all | solution.py:338
  59.1 26.9 %copy-start = (bf16[192,2048]{1,0:T(8,128)(2,1)S(1)}, bf16[192,2048]{1,0:T(8,128)(2,1)}, u32[]{:S(2)}) copy-start(bf16[192,2048]{1,0:T(8,128)(2,1)} %hidden_ref.1) | copy-start | bytes 2359300
  59.1 26.9 %copy-start.1 = (f32[192,128]{1,0:T(8,128)S(1)}, f32[192,128]{1,0:T(8,128)}, u32[]{:S(2)}) copy-start(f32[192,128]{1,0:T(8,128)} %get-tuple-element.26.projected_ref) | copy-start | bytes 294916
  59.1 26.8 %copy-start.2 = (f32[192,128]{1,0:T(8,128)S(1)}, f32[192,128]{1,0:T(8,128)}, u32[]{:S(2)}) copy-start(f32[192,128]{1,0:T(8,128)} %get-tuple-element.25.pair_ref) | copy-start | bytes 294916
  86.9 4.5 %collective-permute-start = (bf16[1024,128]{1,0:T(8,128)(2,1)S(1)}, bf16[1024,128]{1,0:T(8,128)(2,1)S(1)}, u32[]{:S(2)}, u32[]{:S(2)}) collective-permute-start(bf16[1024,128]{1,0:T(8,128)(2,1)S(1)} %get-tuple-element.28), channel_id=1, source_target_pairs={{0,16},{16,0},{1,17},{17,1},{2,18},{18,2},{3,19},{19,3},{4,20},{20... | collective-permute-start | bytes 786440 | tf_op jit(solution)/shard_map/ppermute | solution.py:345

commit v8 on v4

--- a/solution.py
+++ b/solution.py
@@ -209,8 +209,15 @@
     )(place, partial, columns, powers)
 
 
+def half_product(half, hidden_ref, projected_grad):
+    columns = pl.ds(pl.multiple_of(half * HALF, HALF), HALF)
+    return lax.dot_general(
+        hidden_ref[:, columns], projected_grad, (((0,), (0,)), ((), ())), preferred_element_type=jnp.float32
+    )
+
+
 def gradient_body(
-    core_ref, arrived_ref, inverse_ref, pair_ref, projected_ref, hidden_ref, derivative_ref, own_ref, other_ref
+    core_ref, arrived_ref, inverse_ref, pair_ref, projected_ref, hidden_ref, derivative_ref, turned_ref, other_ref
 ):
     sums = jnp.sum(arrived_ref[...].astype(jnp.float32), axis=0)
     mixed = inverse_ref[...] * sums[:, :WIDTH] + sums[:, WIDTH:]
@@ -222,14 +229,30 @@
     alongside = jnp.sum(unit * derivative, axis=1, keepdims=True)
     projected_grad = ((derivative - unit * alongside) * inverse_norm).astype(jnp.bfloat16)
 
-    def product(half):
-        columns = pl.ds(pl.multiple_of(half * HALF, HALF), HALF)
-        return lax.dot_general(
-            hidden_ref[:, columns], projected_grad, (((0,), (0,)), ((), ())), preferred_element_type=jnp.float32
-        )
-
-    own_ref[...] = product(core_ref[0])
-    other_ref[...] = product(1 - core_ref[0]).astype(jnp.bfloat16)
+    turned_ref[...] = projected_grad
+    other_ref[...] = half_product(1 - core_ref[0], hidden_ref, projected_grad).astype(jnp.bfloat16)
+
+
+def own_half_body(core_ref, derivative_ref, turned_ref, hidden_ref, out_ref, own_ref):
+    out_ref[...] = derivative_ref[...]
+    own_ref[...] = half_product(core_ref[0], hidden_ref, turned_ref[...])
+
+
+def own_half(core, derivative, turned, hidden):
+    return pl.pallas_call(
+        own_half_body,
+        in_specs=[SMEM] + [VMEM] * 3,
+        out_specs=(VMEM, VMEM),
+        out_shape=(
+            pltpu.HBM((ROWS, WIDTH), jnp.float32),
+            pltpu.VMEM((HALF, WIDTH), jnp.float32),
+        ),
+        compiler_params=params(16),
+        name="own_half",
+        cost_estimate=pl.CostEstimate(
+            flops=2 * ROWS * HALF * WIDTH, bytes_accessed=4 * ROWS * D_IN, transcendentals=0
+        ),
+    )(core, derivative, turned, hidden)
 
 
 def gradient(core, arrived, inverse, pair, projected, hidden):
@@ -238,8 +261,8 @@
         in_specs=[SMEM] + [VMEM] * 5,
         out_specs=(VMEM,) * 3,
         out_shape=(
-            jax.ShapeDtypeStruct((ROWS, WIDTH), jnp.float32),
-            pltpu.VMEM((HALF, WIDTH), jnp.float32),
+            pltpu.VMEM((ROWS, WIDTH), jnp.float32),
+            pltpu.VMEM((ROWS, WIDTH), jnp.bfloat16),
             pltpu.VMEM((HALF, WIDTH), jnp.bfloat16),
         ),
         compiler_params=params(16),
@@ -341,8 +364,9 @@
     partial = lax.all_to_all(sums, "z", 0, 0)
     weighed, inverse, loss = weigh(place, partial, columns, powers)
     arrived = lax.all_to_all(weighed, PLANE, 0, 0)
-    derivative, own, other = gradient(core, arrived, inverse, pair, projected, hidden)
+    derivative, turned, other = gradient(core, arrived, inverse, pair, projected, hidden)
     other = lax.ppermute(other, "c", [(0, 1), (1, 0)])
+    derivative, own = own_half(core, derivative, turned, hidden)
     shares = lax.all_to_all(join(own, other), PLANE, 0, 0)
     shares = lax.all_to_all(share(shares), "z", 0, 0)
     packets = lax.all_to_all(packet(shares, loss), PLANE, 0, 0)

time: 131 us -> 131 us (level)
  transfers between devices with their start and end apart: 2 -> 2, of which waited for: 1 -> 1; matrix products, arithmetic and copies ran while one was open for 0% -> 0% of each run, Pallas kernels for 0% -> 1%
where the time goes in v8:
time: 131 us; the launch traced here: 130 us
  blocking collectives  100 us (76%)
  Pallas kernels  17.2 us (13%)
  starting transfers between devices  11.5 us (9%)
    all_to_all x1, blocking collectives, local(): arrived = lax.all_to_all(weighed, PLANE, 0, 0)  26.3 us
    all_gather x1, blocking collectives, local(): columns = lax.all_gather(features, COLUMN, axis=0, tiled=True)  22.9 us
    all_to_all x1, blocking collectives, local(): partial = lax.all_to_all(sums, 'z', 0, 0)  11.5 us
    all_to_all x1, blocking collectives, local(): packets = lax.all_to_all(packet(shares, loss), PLANE, 0, 0)  10.8 us
    all_to_all x1, blocking collectives, local(): shares = lax.all_to_all(join(own, other), PLANE, 0, 0)  10.5 us
    all_to_all x1, blocking collectives, local(): shares = lax.all_to_all(share(shares), 'z', 0, 0)  10.4 us
    all_to_all x1, starting transfers between devices, local(): rows = lax.all_to_all(copies, PLANE, 0, 0)  7.6 us
    all_gather x1, blocking collectives, local(): packets = lax.all_gather(packets, 'c', axis=0, tiled=True)  6.14 us
  transfers between devices with their start and end apart: 2, of which 1 were waited for; matrix products, arithmetic and copies ran while one was open for 0% of the time, Pallas kernels for 1%

profile of v8, /device:TPU:1, one launch (start us, length us, event | category | flops | bytes accessed | tf_op | source)
XLA Modules:
  0.0 130.2 jit_solution(16025124539525365444)
XLA Ops:
  0.6 2.7 %project.1 = (f32[192,128]{1,0:T(8,128)}, bf16[192,128]{1,0:T(8,128)(2,1)}, bf16[16,192,128]{2,1,0:T(8,128)(2,1)}, f32[192,128]{1,0:T(8,128)}, f32[8,128]{1,0:T(8,128)}) custom-call(bf16[192,2048]{1,0:T(8,128)(2,1)} %hidden_ref.3, bf16[2048,128]{1,0:T(8,128)(2,1)} %weight_hbm.1, s32[1,192]{1,0:T(1,128)} %bitcast.6), custom_call_target="tpu_custom_call" | custom-call | tf_op jit(solution)/shard_map/project/pallas_call | solution.py:82
  3.4 0.0 copy-start.4
  3.4 0.0 copy-start.3
  3.4 7.6 %all-to-all-start = ((bf16[16,192,128]{2,1,0:T(8,128)(2,1)}), bf16[16,192,128]{2,1,0:T(8,128)(2,1)S(1)}, u32[]{:S(2)}, u32[]{:S(2)}) async-start(bf16[16,192,128]{2,1,0:T(8,128)(2,1)} %get-tuple-element.20), calls=%async_computation | async-start | bytes 1572864 | tf_op jit(solution)/shard_map/all_to_all | solution.py:361
  11.0 0.1 pad_add_fusion.place_ref
  11.1 22.9 %all_gather.9.columns_ref = bf16[3072,128]{1,0:T(8,128)(2,1)S(1)} all-gather(bf16[192,128]{1,0:T(8,128)(2,1)S(1)} %copy-done.4), channel_id=1, replica_groups=mesh['y'=4,'xl'=2,'c'=2,'z'=8,'xh'=2] {'z','c'}, dimensions={0}, use_global_device_ids=true | all-gather | bytes 835584 | tf_op jit(solution)/shard_map/all_gather | solution.py:360
  34.0 0.0 all-to-all-done.rows_ref
  34.0 5.9 %score.1 = (bf16[3072,3072]{1,0:T(8,128)(2,1)S(1)}, f32[32,128]{1,0:T(8,128)S(1)}) custom-call(s32[2]{0:T(128)S(1)} %pad_add_fusion.place_ref, bf16[16,192,128]{2,1,0:T(8,128)(2,1)S(1)} %all-to-all-done.rows_ref, bf16[3072,128]{1,0:T(8,128)(2,1)S(1)} %all_gather.9.columns_ref, f32[8,128]{1,0:T(8,128)S(1)} %copy-done.3), custom_call_target="tpu_custom_call" | custom-call | tf_op jit(solution)/shard_map/score/pallas_call | solution.py:137
  39.9 1.8 %all_gather.10.arrived_ref = f32[64,128]{1,0:T(8,128)S(1)} all-gather(f32[32,128]{1,0:T(8,128)S(1)} %get-tuple-element.23), channel_id=1, replica_groups=mesh['y'=4,'xl'=2,'c'=2,'z'=8,'xh'=2] {'c'}, dimensions={0}, use_global_device_ids=true | all-gather | bytes 49152 | tf_op jit(solution)/shard_map/all_gather | solution.py:363
  41.8 11.5 %all_to_all.30.partial_ref = f32[8,32,128]{2,1,0:T(8,128)S(1)} all-to-all(f32[8,32,128]{2,1,0:T(8,128)S(1)} %spread.1), channel_id=1, replica_groups=mesh['y'=4,'xl'=2,'c'=2,'z'=8,'xh'=2] {'z'}, dimensions={0} | all-to-all | bytes 262144 | tf_op jit(solution)/shard_map/all_to_all | solution.py:364
  53.3 5.8 %weigh.1 = (bf16[16,192,256]{2,1,0:T(8,128)(2,1)S(1)}, f32[192,128]{1,0:T(8,128)S(1)}, f32[8,128]{1,0:T(8,128)S(1)}) custom-call(s32[2]{0:T(128)S(1)} %pad_add_fusion.place_ref, f32[8,32,128]{2,1,0:T(8,128)S(1)} %all_to_all.30.partial_ref, bf16[3072,128]{1,0:T(8,128)(2,1)S(1)} %all_gather.9.columns_ref, bf16[3072,3072]{1,0:T(8,128)(2,1)S(1)} %get-tuple-element.24.powers_ref), custom_call_target="tpu_custom_call" | custom-call | tf_op jit(solution)/shard_map/weigh/pallas_call | solution.py:194
  59.1 0.0 copy-start
  59.1 0.0 copy-start.1
  59.1 26.3 %all_to_all.31.arrived_ref = bf16[16,192,256]{2,1,0:T(8,128)(2,1)S(1)} all-to-all(bf16[16,192,256]{2,1,0:T(8,128)(2,1)S(1)} %get-tuple-element.25), channel_id=1, replica_groups=mesh['y'=4,'xl'=2,'c'=2,'z'=8,'xh'=2] {'y','xl','xh'}, dimensions={0} | all-to-all | bytes 3145728 | tf_op jit(solution)/shard_map/all_to_all | solution.py:366
  85.5 0.0 copy-done.1
  85.5 0.6 gradient.1
  86.1 3.9 %collective-permute-start = (bf16[1024,128]{1,0:T(8,128)(2,1)S(1)}, bf16[1024,128]{1,0:T(8,128)(2,1)S(1)}, u32[]{:S(2)}, u32[]{:S(2)}) collective-permute-start(bf16[1024,128]{1,0:T(8,128)(2,1)S(1)} %get-tuple-element.32), channel_id=1, source_target_pairs={{0,16},{16,0},{1,17},{17,1},{2,18},{18,2},{3,19},{19,3},{4,20},{20... | collective-permute-start | bytes 786440 | tf_op jit(solution)/shard_map/ppermute | solution.py:368
  90.0 0.9 own_half.1
  90.9 0.3 collective-permute-done.other_ref
  91.2 10.5 %all_to_all.32.arrived_ref = bf16[16,64,128]{2,1,0:T(8,128)(2,1)S(1)} all-to-all(bf16[16,64,128]{2,1,0:T(8,128)(2,1)S(1)} %join.1), channel_id=1, replica_groups=mesh['y'=4,'xl'=2,'c'=2,'z'=8,'xh'=2] {'y','xl','xh'}, dimensions={0} | all-to-all | bytes 524288 | tf_op jit(solution)/shard_map/all_to_all | solution.py:370
  101.8 10.4 %all_to_all.33.arrived_ref = bf16[8,64,128]{2,1,0:T(8,128)(2,1)S(1)} all-to-all(bf16[8,64,128]{2,1,0:T(8,128)(2,1)S(1)} %share.1), channel_id=1, replica_groups=mesh['y'=4,'xl'=2,'c'=2,'z'=8,'xh'=2] {'z'}, dimensions={0} | all-to-all | bytes 262144 | tf_op jit(solution)/shard_map/all_to_all | solution.py:371
  112.2 10.8 %all_to_all.34 = bf16[16,80,128]{2,1,0:T(8,128)(2,1)S(1)} all-to-all(bf16[16,80,128]{2,1,0:T(8,128)(2,1)S(1)} %packet.1), channel_id=1, replica_groups=mesh['y'=4,'xl'=2,'c'=2,'z'=8,'xh'=2] {'y','xl','xh'}, dimensions={0} | all-to-all | bytes 655360 | tf_op jit(solution)/shard_map/all_to_all | solution.py:372
  123.0 6.1 %all_gather.11.arrived_ref = bf16[32,80,128]{2,1,0:T(8,128)(2,1)S(1)} all-gather(bf16[16,80,128]{2,1,0:T(8,128)(2,1)S(1)} %all_to_all.34), channel_id=1, replica_groups=mesh['y'=4,'xl'=2,'c'=2,'z'=8,'xh'=2] {'c'}, dimensions={0}, use_global_device_ids=true | all-gather | bytes 983040 | tf_op jit(solution)/shard_map/all_gather | solution.py:373
  129.2 1.0 finish.1
  (9 shorter events, 0.1 us)
Async XLA Ops:
  3.4 7.7 %copy-start.4 = (bf16[192,128]{1,0:T(8,128)(2,1)S(1)}, bf16[192,128]{1,0:T(8,128)(2,1)}, u32[]{:S(2)}) copy-start(bf16[192,128]{1,0:T(8,128)(2,1)} %get-tuple-element.21) | copy-start | bytes 147460
  3.4 30.6 %copy-start.3 = (f32[8,128]{1,0:T(8,128)S(1)}, f32[8,128]{1,0:T(8,128)}, u32[]{:S(2)}) copy-start(f32[8,128]{1,0:T(8,128)} %get-tuple-element.22.pair_sum_ref) | copy-start | bytes 12292
  3.4 30.6 %all-to-all-start = ((bf16[16,192,128]{2,1,0:T(8,128)(2,1)}), bf16[16,192,128]{2,1,0:T(8,128)(2,1)S(1)}, u32[]{:S(2)}, u32[]{:S(2)}) async-start(bf16[16,192,128]{2,1,0:T(8,128)(2,1)} %get-tuple-element.20), calls=%async_computation | async-start | bytes 1572864 | tf_op jit(solution)/shard_map/all_to_all | solution.py:361
  59.1 26.4 %copy-start = (bf16[192,2048]{1,0:T(8,128)(2,1)S(1)}, bf16[192,2048]{1,0:T(8,128)(2,1)}, u32[]{:S(2)}) copy-start(bf16[192,2048]{1,0:T(8,128)(2,1)} %hidden_ref.3) | copy-start | bytes 2359300
  59.1 26.4 %copy-start.1 = (f32[192,128]{1,0:T(8,128)S(1)}, f32[192,128]{1,0:T(8,128)}, u32[]{:S(2)}) copy-start(f32[192,128]{1,0:T(8,128)} %get-tuple-element.28.projected_ref) | copy-start | bytes 294916
  59.1 26.4 %copy-start.2 = (f32[192,128]{1,0:T(8,128)S(1)}, f32[192,128]{1,0:T(8,128)}, u32[]{:S(2)}) copy-start(f32[192,128]{1,0:T(8,128)} %get-tuple-element.27.pair_ref) | copy-start | bytes 294916
  86.1 5.1 %collective-permute-start = (bf16[1024,128]{1,0:T(8,128)(2,1)S(1)}, bf16[1024,128]{1,0:T(8,128)(2,1)S(1)}, u32[]{:S(2)}, u32[]{:S(2)}) collective-permute-start(bf16[1024,128]{1,0:T(8,128)(2,1)S(1)} %get-tuple-element.32), channel_id=1, source_target_pairs={{0,16},{16,0},{1,17},{17,1},{2,18},{18,2},{3,19},{19,3},{4,20},{20... | collective-permute-start | bytes 786440 | tf_op jit(solution)/shard_map/ppermute | solution.py:368

commit v9 on v4

--- a/solution.py
+++ b/solution.py
@@ -247,42 +247,7 @@
     )(core, arrived, inverse, pair, projected, hidden)
 
 
-def join_body(own_ref, other_ref, sum_ref):
-    for k in range(16):
-        part = slice(k * SHARE, (k + 1) * SHARE)
-        sum_ref[k] = (own_ref[part, :] + other_ref[part, :].astype(jnp.float32)).astype(jnp.bfloat16)
-
-
-def join(own, other):
-    return pl.pallas_call(
-        join_body,
-        in_specs=[VMEM] * 2,
-        out_specs=VMEM,
-        out_shape=pltpu.VMEM((16, SHARE, WIDTH), jnp.bfloat16),
-        compiler_params=params(4),
-        name="join",
-    )(own, other)
-
-
-def share_body(arrived_ref, copies_ref):
-    total = jnp.sum(arrived_ref[...].astype(jnp.float32), axis=0).astype(jnp.bfloat16)
-    for k in range(8):
-        copies_ref[k] = total
-
-
-def share(arrived):
-    return pl.pallas_call(
-        share_body,
-        in_specs=[VMEM],
-        out_specs=VMEM,
-        out_shape=pltpu.VMEM((8, SHARE, WIDTH), jnp.bfloat16),
-        compiler_params=params(4),
-        name="share",
-    )(arrived)
-
-
-def packet_body(arrived_ref, loss_ref, copies_ref):
-    total = jnp.sum(arrived_ref[...].astype(jnp.float32), axis=0).astype(jnp.bfloat16)
+def join_body(own_ref, other_ref, loss_ref, sum_ref):
     loss = jnp.broadcast_to(loss_ref[0:1, :], (16, WIDTH))
     high = loss.astype(jnp.bfloat16).astype(jnp.float32)
     middle = (loss - high).astype(jnp.bfloat16).astype(jnp.float32)
@@ -291,37 +256,72 @@
     pieces = jnp.where(row == 0, high, jnp.where(row == 1, middle, jnp.where(row == 2, low, 0.0)))
     pieces = pieces.astype(jnp.bfloat16)
     for k in range(16):
-        copies_ref[k, :SHARE, :] = total
-        copies_ref[k, SHARE:, :] = pieces
-
-
-def packet(arrived, loss):
-    return pl.pallas_call(
-        packet_body,
-        in_specs=[VMEM] * 2,
+        part = slice(k * SHARE, (k + 1) * SHARE)
+        sum_ref[k, SHARE:, :] = pieces
+        sum_ref[k, :SHARE, :] = (own_ref[part, :] + other_ref[part, :].astype(jnp.float32)).astype(jnp.bfloat16)
+
+
+def join(own, other, loss):
+    return pl.pallas_call(
+        join_body,
+        in_specs=[VMEM] * 3,
         out_specs=VMEM,
         out_shape=pltpu.VMEM((16, SHARE + 16, WIDTH), jnp.bfloat16),
+        compiler_params=params(4),
+        name="join",
+    )(own, other, loss)
+
+
+def share_body(arrived_ref, copies_ref, loss_ref):
+    sums = jnp.sum(arrived_ref[...].astype(jnp.float32), axis=0)
+    total = sums[:SHARE, :].astype(jnp.bfloat16)
+    loss_ref[...] = jnp.sum(sums[SHARE:, 0:1], axis=0, keepdims=True) * (1.0 / (256 * ROWS))
+    for k in range(8):
+        copies_ref[k] = total
+
+
+def share(arrived):
+    return pl.pallas_call(
+        share_body,
+        in_specs=[VMEM],
+        out_specs=(VMEM, VMEM),
+        out_shape=(
+            pltpu.VMEM((8, SHARE, WIDTH), jnp.bfloat16),
+            jax.ShapeDtypeStruct((1, 1), jnp.float32),
+        ),
+        compiler_params=params(4),
+        name="share",
+    )(arrived)
+
+
+def packet_body(arrived_ref, copies_ref):
+    total = jnp.sum(arrived_ref[...].astype(jnp.float32), axis=0).astype(jnp.bfloat16)
+    for k in range(16):
+        copies_ref[k] = total
+
+
+def packet(arrived):
+    return pl.pallas_call(
+        packet_body,
+        in_specs=[VMEM],
+        out_specs=VMEM,
+        out_shape=pltpu.VMEM((16, SHARE, WIDTH), jnp.bfloat16),
         compiler_params=params(8),
         name="packet",
-    )(arrived, loss)
-
-
-def finish_body(arrived_ref, loss_ref, grad_ref):
+    )(arrived)
+
+
+def finish_body(arrived_ref, grad_ref):
     for k in range(32):
-        grad_ref[k] = arrived_ref[k, :SHARE, :].astype(jnp.float32)
-    pieces = jnp.sum(arrived_ref[:, SHARE:, :].astype(jnp.float32), axis=0)
-    loss_ref[...] = jnp.sum(pieces[:, 0:1], axis=0, keepdims=True) * (0.5 / (256 * ROWS))
+        grad_ref[k] = arrived_ref[k].astype(jnp.float32)
 
 
 def finish(arrived):
     return pl.pallas_call(
         finish_body,
         in_specs=[VMEM],
-        out_specs=(VMEM, VMEM),
-        out_shape=(
-            jax.ShapeDtypeStruct((1, 1), jnp.float32),
-            jax.ShapeDtypeStruct((32, SHARE, WIDTH), jnp.float32),
-        ),
+        out_specs=VMEM,
+        out_shape=jax.ShapeDtypeStruct((32, SHARE, WIDTH), jnp.float32),
         compiler_params=params(8),
         name="finish",
     )(arrived)
@@ -343,11 +343,12 @@
     arrived = lax.all_to_all(weighed, PLANE, 0, 0)
     derivative, own, other = gradient(core, arrived, inverse, pair, projected, hidden)
     other = lax.ppermute(other, "c", [(0, 1), (1, 0)])
-    shares = lax.all_to_all(join(own, other), PLANE, 0, 0)
-    shares = lax.all_to_all(share(shares), "z", 0, 0)
-    packets = lax.all_to_all(packet(shares, loss), PLANE, 0, 0)
+    shares = lax.all_to_all(join(own, other, loss), PLANE, 0, 0)
+    shares, mean_loss = share(shares)
+    shares = lax.all_to_all(shares, "z", 0, 0)
+    packets = lax.all_to_all(packet(shares), PLANE, 0, 0)
     packets = lax.all_gather(packets, "c", axis=0, tiled=True)
-    mean_loss, grad_weight = finish(packets)
+    grad_weight = finish(packets)
     return (mean_loss.reshape(()), derivative, grad_weight.reshape(D_IN, WIDTH))
 
 

time: 131 us -> 132 us (level)
  no operation moved by 1% of the time
where the time goes in v9:
time: 132 us; the launch traced here: 131 us
  blocking collectives  101 us (77%)
  Pallas kernels  17.1 us (13%)
  starting transfers between devices  11.4 us (9%)
    all_to_all x1, blocking collectives, local(): arrived = lax.all_to_all(weighed, PLANE, 0, 0)  26.3 us
    all_gather x1, blocking collectives, local(): columns = lax.all_gather(features, COLUMN, axis=0, tiled=True)  22.9 us
    all_to_all x1, blocking collectives, local(): partial = lax.all_to_all(sums, 'z', 0, 0)  11.5 us
    all_to_all x1, blocking collectives, local(): packets = lax.all_to_all(packet(shares), PLANE, 0, 0)  10.9 us
    all_to_all x1, blocking collectives, local(): shares = lax.all_to_all(join(own, other, loss), PLANE, 0, 0)  10.9 us
    all_to_all x1, blocking collectives, local(): shares = lax.all_to_all(shares, 'z', 0, 0)  10.4 us
    all_to_all x1, starting transfers between devices, local(): rows = lax.all_to_all(copies, PLANE, 0, 0)  7.6 us
    all_gather x1, blocking collectives, local(): packets = lax.all_gather(packets, 'c', axis=0, tiled=True)  6.05 us
  transfers between devices with their start and end apart: 2, of which 1 were waited for; matrix products, arithmetic and copies ran while one was open for 0% of the time, Pallas kernels for 0%

profile of v9, /device:TPU:1, one launch (start us, length us, event | category | flops | bytes accessed | tf_op | source)
XLA Modules:
  0.0 131.2 jit_solution(14470745680179321784)
XLA Ops:
  0.6 2.8 %project.1 = (f32[192,128]{1,0:T(8,128)}, bf16[192,128]{1,0:T(8,128)(2,1)}, bf16[16,192,128]{2,1,0:T(8,128)(2,1)}, f32[192,128]{1,0:T(8,128)}, f32[8,128]{1,0:T(8,128)}) custom-call(bf16[192,2048]{1,0:T(8,128)(2,1)} %hidden_ref.1, bf16[2048,128]{1,0:T(8,128)(2,1)} %weight_hbm.1, s32[1,192]{1,0:T(1,128)} %bitcast.7), custom_call_target="tpu_custom_call" | custom-call | tf_op jit(solution)/shard_map/project/pallas_call | solution.py:82
  3.4 0.0 copy-start.4
  3.4 0.0 copy-start.3
  3.4 7.6 %all-to-all-start = ((bf16[16,192,128]{2,1,0:T(8,128)(2,1)}), bf16[16,192,128]{2,1,0:T(8,128)(2,1)S(1)}, u32[]{:S(2)}, u32[]{:S(2)}) async-start(bf16[16,192,128]{2,1,0:T(8,128)(2,1)} %get-tuple-element.18), calls=%async_computation | async-start | bytes 1572864 | tf_op jit(solution)/shard_map/all_to_all | solution.py:338
  11.0 0.1 pad_add_fusion.place_ref
  11.1 0.0 copy-done.4
  11.1 22.9 %all_gather.9.columns_ref = bf16[3072,128]{1,0:T(8,128)(2,1)S(1)} all-gather(bf16[192,128]{1,0:T(8,128)(2,1)S(1)} %copy-done.4), channel_id=1, replica_groups=mesh['y'=4,'xl'=2,'c'=2,'z'=8,'xh'=2] {'z','c'}, dimensions={0}, use_global_device_ids=true | all-gather | bytes 835584 | tf_op jit(solution)/shard_map/all_gather | solution.py:337
  34.0 0.0 all-to-all-done.rows_ref
  34.0 5.9 %score.1 = (bf16[3072,3072]{1,0:T(8,128)(2,1)S(1)}, f32[32,128]{1,0:T(8,128)S(1)}) custom-call(s32[2]{0:T(128)S(1)} %pad_add_fusion.place_ref, bf16[16,192,128]{2,1,0:T(8,128)(2,1)S(1)} %all-to-all-done.rows_ref, bf16[3072,128]{1,0:T(8,128)(2,1)S(1)} %all_gather.9.columns_ref, f32[8,128]{1,0:T(8,128)S(1)} %copy-done.3), custom_call_target="tpu_custom_call" | custom-call | tf_op jit(solution)/shard_map/score/pallas_call | solution.py:137
  39.9 1.8 %all_gather.10.arrived_ref = f32[64,128]{1,0:T(8,128)S(1)} all-gather(f32[32,128]{1,0:T(8,128)S(1)} %get-tuple-element.21), channel_id=1, replica_groups=mesh['y'=4,'xl'=2,'c'=2,'z'=8,'xh'=2] {'c'}, dimensions={0}, use_global_device_ids=true | all-gather | bytes 49152 | tf_op jit(solution)/shard_map/all_gather | solution.py:340
  41.8 11.5 %all_to_all.30.partial_ref = f32[8,32,128]{2,1,0:T(8,128)S(1)} all-to-all(f32[8,32,128]{2,1,0:T(8,128)S(1)} %spread.1), channel_id=1, replica_groups=mesh['y'=4,'xl'=2,'c'=2,'z'=8,'xh'=2] {'z'}, dimensions={0} | all-to-all | bytes 262144 | tf_op jit(solution)/shard_map/all_to_all | solution.py:341
  53.3 5.8 %weigh.1 = (bf16[16,192,256]{2,1,0:T(8,128)(2,1)S(1)}, f32[192,128]{1,0:T(8,128)S(1)}, f32[8,128]{1,0:T(8,128)S(1)}) custom-call(s32[2]{0:T(128)S(1)} %pad_add_fusion.place_ref, f32[8,32,128]{2,1,0:T(8,128)S(1)} %all_to_all.30.partial_ref, bf16[3072,128]{1,0:T(8,128)(2,1)S(1)} %all_gather.9.columns_ref, bf16[3072,3072]{1,0:T(8,128)(2,1)S(1)} %get-tuple-element.22.powers_ref), custom_call_target="tpu_custom_call" | custom-call | tf_op jit(solution)/shard_map/weigh/pallas_call | solution.py:194
  59.1 0.0 copy-start
  59.1 0.0 copy-start.1
  59.1 26.3 %all_to_all.31.arrived_ref = bf16[16,192,256]{2,1,0:T(8,128)(2,1)S(1)} all-to-all(bf16[16,192,256]{2,1,0:T(8,128)(2,1)S(1)} %get-tuple-element.23), channel_id=1, replica_groups=mesh['y'=4,'xl'=2,'c'=2,'z'=8,'xh'=2] {'y','xl','xh'}, dimensions={0} | all-to-all | bytes 3145728 | tf_op jit(solution)/shard_map/all_to_all | solution.py:343
  85.5 0.9 gradient.1
  86.4 3.8 %collective-permute-start = (bf16[1024,128]{1,0:T(8,128)(2,1)S(1)}, bf16[1024,128]{1,0:T(8,128)(2,1)S(1)}, u32[]{:S(2)}, u32[]{:S(2)}) collective-permute-start(bf16[1024,128]{1,0:T(8,128)(2,1)S(1)} %get-tuple-element.28), channel_id=1, source_target_pairs={{0,16},{16,0},{1,17},{17,1},{2,18},{18,2},{3,19},{19,3},{4,20},{20... | collective-permute-start | bytes 786440 | tf_op jit(solution)/shard_map/ppermute | solution.py:345
  90.2 1.2 collective-permute-done.other_ref
  91.4 10.9 %all_to_all.32.arrived_ref = bf16[16,80,128]{2,1,0:T(8,128)(2,1)S(1)} all-to-all(bf16[16,80,128]{2,1,0:T(8,128)(2,1)S(1)} %join.1), channel_id=1, replica_groups=mesh['y'=4,'xl'=2,'c'=2,'z'=8,'xh'=2] {'y','xl','xh'}, dimensions={0} | all-to-all | bytes 655360 | tf_op jit(solution)/shard_map/all_to_all | solution.py:346
  102.3 0.5 share.1
  102.8 10.4 %all_to_all.33.arrived_ref = bf16[8,64,128]{2,1,0:T(8,128)(2,1)S(1)} all-to-all(bf16[8,64,128]{2,1,0:T(8,128)(2,1)S(1)} %get-tuple-element.32), channel_id=1, replica_groups=mesh['y'=4,'xl'=2,'c'=2,'z'=8,'xh'=2] {'z'}, dimensions={0} | all-to-all | bytes 262144 | tf_op jit(solution)/shard_map/all_to_all | solution.py:348
  113.3 10.9 %all_to_all.34 = bf16[16,64,128]{2,1,0:T(8,128)(2,1)S(1)} all-to-all(bf16[16,64,128]{2,1,0:T(8,128)(2,1)S(1)} %packet.1), channel_id=1, replica_groups=mesh['y'=4,'xl'=2,'c'=2,'z'=8,'xh'=2] {'y','xl','xh'}, dimensions={0} | all-to-all | bytes 524288 | tf_op jit(solution)/shard_map/all_to_all | solution.py:349
  124.2 6.1 %all_gather.11.arrived_ref = bf16[32,64,128]{2,1,0:T(8,128)(2,1)S(1)} all-gather(bf16[16,64,128]{2,1,0:T(8,128)(2,1)S(1)} %all_to_all.34), channel_id=1, replica_groups=mesh['y'=4,'xl'=2,'c'=2,'z'=8,'xh'=2] {'c'}, dimensions={0}, use_global_device_ids=true | all-gather | bytes 786432 | tf_op jit(solution)/shard_map/all_gather | solution.py:350
  130.2 1.0 finish.1
  (8 shorter events, 0.1 us)
Async XLA Ops:
  3.4 7.7 %copy-start.4 = (bf16[192,128]{1,0:T(8,128)(2,1)S(1)}, bf16[192,128]{1,0:T(8,128)(2,1)}, u32[]{:S(2)}) copy-start(bf16[192,128]{1,0:T(8,128)(2,1)} %get-tuple-element.19) | copy-start | bytes 147460
  3.4 30.6 %copy-start.3 = (f32[8,128]{1,0:T(8,128)S(1)}, f32[8,128]{1,0:T(8,128)}, u32[]{:S(2)}) copy-start(f32[8,128]{1,0:T(8,128)} %get-tuple-element.20.pair_sum_ref) | copy-start | bytes 12292
  3.4 30.6 %all-to-all-start = ((bf16[16,192,128]{2,1,0:T(8,128)(2,1)}), bf16[16,192,128]{2,1,0:T(8,128)(2,1)S(1)}, u32[]{:S(2)}, u32[]{:S(2)}) async-start(bf16[16,192,128]{2,1,0:T(8,128)(2,1)} %get-tuple-element.18), calls=%async_computation | async-start | bytes 1572864 | tf_op jit(solution)/shard_map/all_to_all | solution.py:338
  59.1 26.4 %copy-start = (bf16[192,2048]{1,0:T(8,128)(2,1)S(1)}, bf16[192,2048]{1,0:T(8,128)(2,1)}, u32[]{:S(2)}) copy-start(bf16[192,2048]{1,0:T(8,128)(2,1)} %hidden_ref.1) | copy-start | bytes 2359300
  59.1 26.4 %copy-start.1 = (f32[192,128]{1,0:T(8,128)S(1)}, f32[192,128]{1,0:T(8,128)}, u32[]{:S(2)}) copy-start(f32[192,128]{1,0:T(8,128)} %get-tuple-element.26.projected_ref) | copy-start | bytes 294916
  59.1 26.4 %copy-start.2 = (f32[192,128]{1,0:T(8,128)S(1)}, f32[192,128]{1,0:T(8,128)}, u32[]{:S(2)}) copy-start(f32[192,128]{1,0:T(8,128)} %get-tuple-element.25.pair_ref) | copy-start | bytes 294916
  86.4 5.0 %collective-permute-start = (bf16[1024,128]{1,0:T(8,128)(2,1)S(1)}, bf16[1024,128]{1,0:T(8,128)(2,1)S(1)}, u32[]{:S(2)}, u32[]{:S(2)}) collective-permute-start(bf16[1024,128]{1,0:T(8,128)(2,1)S(1)} %get-tuple-element.28), channel_id=1, source_target_pairs={{0,16},{16,0},{1,17},{17,1},{2,18},{18,2},{3,19},{19,3},{4,20},{20... | collective-permute-start | bytes 786440 | tf_op jit(solution)/shard_map/ppermute | solution.py:345
